TPU v7x, 256 devices: a whole 4x4x8 slice. The times are simulated.
256 devices in a mesh: gx: 8 (over z_lo, x), gy: 32 (over z_hi, y, core).
Axes of the slice: x: 4, y: 4, z: 8 (z_hi: 4, z_lo: 2; z = z_hi * 2 + z_lo), core: 2. Of those that a mesh axis runs over, the one named last changes fastest.
Arguments:
- snapshot: float32 [384, 384, 32, 16], P('gx', 'gy'), may hold values from -6 to 6
- start_x: float32 [384, 96], replicated, may hold values from -0.3125 to 0.3125
- start_y: float32 [384, 96], replicated, may hold values from -0.3125 to 0.3125
Outputs:
- basis_x: float32 [384, 96], P('gx')
- basis_y: float32 [384, 96], P('gy')
- core: float32 [96, 96, 32, 16], P('gx', 'gy')
All inputs are finite; a program needn't handle non-finite values.
Results may differ from a plain program's by a relative error of at most 0.0003.
Values sent between devices are 32-bit elements; how exact they have to be, the bound alone decides.
A program may use at most 64 MiB of HBM per device.

v0:
```python
import jax
import jax.numpy as jnp
from jax import lax
from jax.sharding import PartitionSpec as P

ITERS = 4


HIGH = lax.Precision.HIGHEST


def normalize(matrix, cross):
    lower = jnp.linalg.cholesky(cross)
    return lax.linalg.triangular_solve(lower, matrix, left_side=False, lower=True, transpose_a=True)


def iterate_x(gram_rows, start):
    own = start
    for step in range(ITERS):
        full = start if step == 0 else lax.all_gather(own, "gx", axis=0, tiled=True)
        image = jnp.dot(gram_rows, full, precision=HIGH)
        cross = lax.psum(jnp.dot(image.T, image, precision=HIGH), "gx")
        own = normalize(image, cross)
    return own


def iterate_y(gram_rows, start):
    own = start
    for step in range(ITERS):
        full = start if step == 0 else lax.all_gather(own, "gy", axis=0, tiled=True)
        image = jnp.dot(gram_rows, full, precision=HIGH)
        cross = lax.psum(jnp.dot(image.T, image, precision=HIGH), "gy")
        own = normalize(image, cross)
    return own


def local(snapshot, start_x, start_y):
    rows_x, rows_y, cells_z, nvars = snapshot.shape
    flat = snapshot.reshape(rows_x, rows_y * cells_z * nvars)
    block = jnp.dot(flat, lax.all_gather(flat, "gx", axis=0, tiled=True).T, precision=HIGH)
    gram_x = lax.psum(block, "gy")
    basis_x = iterate_x(gram_x, start_x)
    chosen = basis_x
    reduced = lax.psum_scatter(
        jnp.dot(chosen.T, flat, precision=HIGH), "gx", scatter_dimension=0, tiled=True
    )
    ranks = reduced.shape[0]
    cube = reduced.reshape(ranks, rows_y, cells_z * nvars)
    planes = lax.all_to_all(cube, "gy", split_axis=2, concat_axis=1, tiled=True)
    whole_y = jnp.einsum("ryc,rwc->yw", planes, planes, precision=HIGH)
    partial_y = lax.psum_scatter(whole_y, "gy", scatter_dimension=0, tiled=True)
    gram_y = lax.psum(partial_y, "gx")
    basis_y = iterate_y(gram_y, start_y)
    chosen = basis_y
    core_part = lax.psum_scatter(
        jnp.einsum("ys,ryc->src", chosen, cube, precision=HIGH),
        "gy",
        scatter_dimension=0,
        tiled=True,
    )
    kept = core_part.shape[0]
    core = jnp.transpose(core_part, (1, 0, 2)).reshape(ranks, kept, cells_z, nvars)
    return (basis_x, basis_y, core)


def solution(mesh):
    in_specs = (P("gx", "gy", None, None), P(), P())
    out_specs = (P("gx", None), P("gy", None), P("gx", "gy", None, None))
    return jax.shard_map(local, mesh=mesh, in_specs=in_specs, out_specs=out_specs, check_vma=False)
```

profile of v0, /device:TPU:57, one launch (start us, length us, event | category | flops | bytes accessed | tf_op | source)
XLA Modules:
  0.0 1749.8 jit_solution(11043200647897753276)
XLA Ops:
  10.6 105.7 %all-gather.5.cloned.1.call-done = f32[384,6144]{1,0:T(8,128)} async-done(((f32[48,6144]{1,0:T(8,128)}), f32[384,6144]{1,0:T(8,128)}) %all-gather.5.cloned.1.call-update) | async-done | bytes 9437200 | tf_op jit(solution)/shard_map/all_gather | solution.py:40
  116.3 13.4 fusion.35
  129.8 245.5 %all-reduce.6.cloned.1.call-done = f32[48,384]{1,0:T(8,128)} async-done(((f32[48,384]{1,0:T(8,128)}), f32[48,384]{1,0:T(8,128)}) %all-reduce.6.cloned.1.call-update) | async-done | bytes 73744 | tf_op jit(solution)/shard_map/psum | solution.py:41
  376.7 27.2 %psum.71 = f32[96,96]{0,1:T(8,128)S(1)} all-reduce(f32[96,96]{0,1:T(8,128)S(1)} %fusion.37), channel_id=1, replica_groups=mesh['gx'=8,'gy'=32] {'gx'}, use_global_device_ids=true, to_apply=%region_1.0 | all-reduce | flops 9216 | bytes 73728 | tf_op jit(solution)/shard_map/psum | solution.py:22
  404.0 8.8 cholesky.134
  421.7 21.9 %all_gather.22 = f32[384,96]{1,0:T(8,128)S(1)} all-gather(f32[48,96]{1,0:T(8,128)S(1)} %convolution_bitcast_fusion.4), channel_id=1, replica_groups=mesh['gx'=8,'gy'=32] {'gx'}, dimensions={0}, use_global_device_ids=true | all-gather | bytes 165888 | tf_op jit(solution)/shard_map/all_gather | solution.py:20
  445.0 24.8 %psum.72 = f32[96,96]{0,1:T(8,128)S(1)} all-reduce(f32[96,96]{0,1:T(8,128)S(1)} %fusion.39), channel_id=1, replica_groups=mesh['gx'=8,'gy'=32] {'gx'}, use_global_device_ids=true, to_apply=%region_4.7 | all-reduce | flops 9216 | bytes 73728 | tf_op jit(solution)/shard_map/psum | solution.py:22
  469.9 8.8 cholesky.145
  487.6 21.9 %all_gather.23 = f32[384,96]{1,0:T(8,128)S(1)} all-gather(f32[48,96]{1,0:T(8,128)S(1)} %convolution_bitcast_fusion.3), channel_id=1, replica_groups=mesh['gx'=8,'gy'=32] {'gx'}, dimensions={0}, use_global_device_ids=true | all-gather | bytes 165888 | tf_op jit(solution)/shard_map/all_gather | solution.py:20
  510.9 25.2 %psum.73 = f32[96,96]{0,1:T(8,128)S(1)} all-reduce(f32[96,96]{0,1:T(8,128)S(1)} %fusion.41), channel_id=1, replica_groups=mesh['gx'=8,'gy'=32] {'gx'}, use_global_device_ids=true, to_apply=%region_5.8 | all-reduce | flops 9216 | bytes 73728 | tf_op jit(solution)/shard_map/psum | solution.py:22
  536.2 8.8 cholesky.156
  553.9 21.9 %all_gather.24 = f32[384,96]{1,0:T(8,128)S(1)} all-gather(f32[48,96]{1,0:T(8,128)S(1)} %convolution_bitcast_fusion.2), channel_id=1, replica_groups=mesh['gx'=8,'gy'=32] {'gx'}, dimensions={0}, use_global_device_ids=true | all-gather | bytes 165888 | tf_op jit(solution)/shard_map/all_gather | solution.py:20
  576.3 25.1 %psum.74 = f32[96,96]{0,1:T(8,128)S(1)} all-reduce(f32[96,96]{0,1:T(8,128)S(1)} %fusion.43), channel_id=1, replica_groups=mesh['gx'=8,'gy'=32] {'gx'}, use_global_device_ids=true, to_apply=%region_6.9 | all-reduce | flops 9216 | bytes 73728 | tf_op jit(solution)/shard_map/psum | solution.py:22
  601.5 8.8 cholesky.167
  623.8 25.4 %fusion = f32[16,6144]{1,0:T(8,128)S(1)} fusion(f32[96,6144]{1,0:T(8,128)} %fusion.44), kind=kCustom, calls=%all-reduce-scatter | all-reduce-scatter fusion | flops 786433 | bytes 2753536
  655.1 9.0 collective-permute-done.1
  672.6 75.6 %all_to_all.18 = f32[32,1,2304]{2,1,0:T(1,128)S(1)} all-to-all(f32[32,1,2304]{2,1,0:T(1,128)S(1)} %reshape.73), channel_id=1, replica_groups=mesh['gx'=8,'gy'=32] {'gy'}, dimensions={0} | all-to-all | bytes 589824 | tf_op jit(solution)/shard_map/all_to_all | solution.py:49
  762.6 63.9 %fusion.1 = f32[16,384]{1,0:T(8,128)S(1)} fusion(f32[384,384]{1,0:T(8,128)S(1)} %convolution_bitcast_fusion), kind=kCustom, calls=%all-reduce-scatter.1 | all-reduce-scatter fusion | flops 196609 | bytes 615424
  835.8 13.7 collective-permute-start.9
  867.6 25.1 %psum.75 = f32[12,384]{1,0:T(8,128)S(1)} all-reduce(f32[12,384]{1,0:T(8,128)S(1)} %constant_dynamic-slice_fusion), channel_id=1, replica_groups=mesh['gx'=8,'gy'=32] {'gx'}, use_global_device_ids=true, to_apply=%region_9.12 | all-reduce | flops 4608 | bytes 36864 | tf_op jit(solution)/shard_map/psum | solution.py:52
  893.2 122.4 %psum.76 = f32[96,96]{0,1:T(8,128)S(1)} all-reduce(f32[96,96]{0,1:T(8,128)S(1)} %fusion.46), channel_id=1, replica_groups=mesh['gx'=8,'gy'=32] {'gy'}, use_global_device_ids=true, to_apply=%region_10.13 | all-reduce | flops 9216 | bytes 73728 | tf_op jit(solution)/shard_map/psum | solution.py:32
  1015.7 8.8 cholesky.178
  1033.3 58.2 %all-gather = f32[32,12,96]{2,1,0:T(8,128)S(1)} all-gather(f32[1,12,96]{2,1,0:T(8,128)S(1)} %convolution_bitcast_fusion.7), channel_id=1, replica_groups=mesh['gx'=8,'gy'=32] {'gy'}, dimensions={0}, use_global_device_ids=true | all-gather | bytes 152064 | tf_op jit(solution)/shard_map/all_gather | solution.py:30
  1092.0 120.5 %psum.77 = f32[96,96]{0,1:T(8,128)S(1)} all-reduce(f32[96,96]{0,1:T(8,128)S(1)} %fusion.48), channel_id=1, replica_groups=mesh['gx'=8,'gy'=32] {'gy'}, use_global_device_ids=true, to_apply=%region_11.15 | all-reduce | flops 9216 | bytes 73728 | tf_op jit(solution)/shard_map/psum | solution.py:32
  1212.6 8.8 cholesky.189
  1230.2 59.1 %all-gather.1 = f32[32,12,96]{2,1,0:T(8,128)S(1)} all-gather(f32[1,12,96]{2,1,0:T(8,128)S(1)} %convolution_bitcast_fusion.6), channel_id=1, replica_groups=mesh['gx'=8,'gy'=32] {'gy'}, dimensions={0}, use_global_device_ids=true | all-gather | bytes 152064 | tf_op jit(solution)/shard_map/all_gather | solution.py:30
  1289.8 120.8 %psum.78 = f32[96,96]{0,1:T(8,128)S(1)} all-reduce(f32[96,96]{0,1:T(8,128)S(1)} %fusion.50), channel_id=1, replica_groups=mesh['gx'=8,'gy'=32] {'gy'}, use_global_device_ids=true, to_apply=%region_12.16 | all-reduce | flops 9216 | bytes 73728 | tf_op jit(solution)/shard_map/psum | solution.py:32
  1410.7 8.8 cholesky.200
  1428.3 59.1 %all-gather.2 = f32[32,12,96]{2,1,0:T(8,128)S(1)} all-gather(f32[1,12,96]{2,1,0:T(8,128)S(1)} %convolution_bitcast_fusion.5), channel_id=1, replica_groups=mesh['gx'=8,'gy'=32] {'gy'}, dimensions={0}, use_global_device_ids=true | all-gather | bytes 152064 | tf_op jit(solution)/shard_map/all_gather | solution.py:30
  1488.0 120.5 %psum.79 = f32[96,96]{0,1:T(8,128)S(1)} all-reduce(f32[96,96]{0,1:T(8,128)S(1)} %fusion.52), channel_id=1, replica_groups=mesh['gx'=8,'gy'=32] {'gy'}, use_global_device_ids=true, to_apply=%region_13.17 | all-reduce | flops 9216 | bytes 73728 | tf_op jit(solution)/shard_map/psum | solution.py:32
  1608.6 8.8 cholesky.211
  1631.4 109.4 %reduce-scatter.6.cloned.1.call-done = f32[3,12,512]{2,1,0:T(8,128)} async-done(((f32[96,12,512]{2,1,0:T(8,128)}), f32[3,12,512]{2,1,0:T(8,128)}) %reduce-scatter.6.cloned.1.call-update) | async-done | bytes 73744 | tf_op jit(solution)/shard_map/reduce_scatter | solution.py:55
  (142 shorter events, 148.2 us)
Async XLA Ops:
  7.2 368.1 %copy-start = (f32[384,96]{0,1:T(8,128)S(1)}, f32[384,96]{0,1:T(8,128)}, u32[]{:S(2)}) copy-start(f32[384,96]{0,1:T(8,128)} %param.9) | copy-start | bytes 442372
  7.2 109.1 %copy-start.1 = (f32[48,12,32,16]{0,3,2,1:T(8,128)S(1)}, f32[48,12,32,16]{0,3,2,1:T(8,128)}, u32[]{:S(2)}) copy-start(f32[48,12,32,16]{0,3,2,1:T(8,128)} %param.8) | copy-start | bytes 3538948
  7.2 109.1 %all-gather.5.cloned.1.call-start = ((), (), s32[]{:S(2)}) async-start(), calls=%async_computation.2 | async-start | bytes 10616832 | tf_op jit(solution)/shard_map/all_gather | solution.py:40
  10.6 364.7 %all-reduce.6.cloned.1.call-start = ((), (), s32[]{:S(2)}) async-start(), calls=%async_computation.3 | async-start | bytes 147456 | tf_op jit(solution)/shard_map/psum | solution.py:41
  129.7 1611.0 %reduce-scatter.6.cloned.1.call-start = ((), (), s32[]{:S(2)}) async-start(), calls=%async_computation.4 | async-start | bytes 3244032 | tf_op jit(solution)/shard_map/reduce_scatter | solution.py:55
  375.2 200.6 %copy-start.4 = (f32[48,384]{1,0:T(8,128)S(1)}, f32[48,384]{1,0:T(8,128)}, u32[]{:S(2)}) copy-start(f32[48,384]{1,0:T(8,128)} %all-reduce.6.cloned.1.call-done) | copy-start | bytes 221188
  619.2 30.1 %copy-start.6 = (f32[48,96]{1,0:T(8,128)}, f32[48,96]{1,0:T(8,128)S(1)}, u32[]{:S(2)}) copy-start(f32[48,96]{1,0:T(8,128)S(1)} %convolution_bitcast_fusion.1) | copy-start | bytes 55300
  623.8 30.1 %copy-start.9 = (u32[256]{0:T(256)S(1)}, u32[256]{0:T(256)}, u32[]{:S(2)}) copy-start(u32[256]{0:T(256)} %constant.35) | copy-start | bytes 3076
  649.2 14.8 collective-permute-start
  651.2 12.9 collective-permute-start.1
  665.3 7.3 copy-start.2
  757.3 104.9 %copy-start.8 = (u32[256]{0:T(256)S(1)}, u32[256]{0:T(256)}, u32[]{:S(2)}) copy-start(u32[256]{0:T(256)} %constant.39) | copy-start | bytes 3076
  757.3 135.4 %copy-start.5 = (f32[384,96]{0,1:T(8,128)S(1)}, f32[384,96]{0,1:T(8,128)}, u32[]{:S(2)}) copy-start(f32[384,96]{0,1:T(8,128)} %param.10) | copy-start | bytes 442372
  826.5 799.7 %copy-start.3 = (f32[12,12,512]{2,1,0:T(8,128)S(1)}, f32[12,12,512]{2,1,0:T(8,128)}, u32[]{:S(2)}) copy-start(f32[12,12,512]{2,1,0:T(8,128)} %copy-done.2) | copy-start | bytes 884740
  826.5 31.8 %collective-permute-start.2 = (f32[16,384]{1,0:T(8,128)S(1)}, f32[16,384]{1,0:T(8,128)S(1)}, u32[]{:S(2)}, u32[]{:S(2)}) collective-permute-start(f32[16,384]{1,0:T(8,128)S(1)} %fusion.1), channel_id=1, source_target_pairs={{0,1},{1,2},{2,3},{3,4},{4,5},{5,6},{6,7},{7,8},{8,9},{9,10},{10,1... | collective-permute-start | bytes 73736
  833.9 26.4 %collective-permute-start.3 = (f32[16,384]{1,0:T(8,128)S(1)}, f32[16,384]{1,0:T(8,128)S(1)}, u32[]{:S(2)}, u32[]{:S(2)}) collective-permute-start(f32[16,384]{1,0:T(8,128)S(1)} %fusion.1), channel_id=1, source_target_pairs={{0,2},{1,3},{2,4},{3,5},{4,6},{5,7},{6,8},{7,9},{8,10},{9,11},{10,... | collective-permute-start | bytes 73736
  835.8 20.5 %collective-permute-start.9 = (f32[12,384]{1,0:T(8,128)S(1)}, f32[12,384]{1,0:T(8,128)S(1)}, u32[]{:S(2)}, u32[]{:S(2)}) collective-permute-start(f32[12,384]{1,0:T(8,128)S(1)} %slice.9), channel_id=1, source_target_pairs={{0,8},{1,9},{2,10},{3,11},{4,12},{5,13},{6,14},{7,15},{8,16},{9,17... | collective-permute-start | bytes 55304
  849.6 13.9 collective-permute-start.4
  851.5 12.0 collective-permute-start.5
  856.4 7.1 collective-permute-start.6
  858.3 5.8 collective-permute-start.7
  860.3 6.4 collective-permute-start.8
  1626.2 5.1 copy-start.7
Sparse Core Ops, SparseCore 0:
  10.7 105.5 all-gather.4
  129.8 245.3 all-reduce.5
  1631.5 109.1 reduce-scatter.5
where the time goes:
time: 1760 us; the launch traced here: 1750 us
  blocking collectives  1020 us (58%)
  waiting for transfers between devices  473 us (27%)
  other arithmetic  141 us (8%)
  starting transfers between devices  40.2 us (2%)
  local copies, waits for them, and re-layouts  30.9 us (2%)
  matrix products  30 us (2%)
    psum x4, blocking collectives, iterate_y(): cross = lax.psum(jnp.dot(image.T, image, precision=HIGH), 'gy')  484 us
    psum x1, waiting for transfers between devices, local(): gram_x = lax.psum(block, 'gy')  245 us
    all_gather x3, blocking collectives, iterate_y(): full = start if step == 0 else lax.all_gather(own, 'gy', axis=0, tiled=True)  176 us
    reduce_scatter x1, waiting for transfers between devices, local(): lax.psum_scatter(jnp.einsum('ys,ryc->src', chosen, cube, precision=HIGH),...  109 us
    all_gather x1, waiting for transfers between devices, local(): lax.all_gather(flat, 'gx', axis=0, tiled=True)  106 us
    psum x4, blocking collectives, iterate_x(): cross = lax.psum(jnp.dot(image.T, image, precision=HIGH), 'gx')  102 us
    unnamed x2, blocking collectives  89.3 us
    another operation x24, other arithmetic, normalize(): lower = jnp.linalg.cholesky(cross)  75.6 us
  transfers between devices with their start and end apart: 13, of which 6 were waited for; matrix products, arithmetic and copies ran while one was open for 0% of the time, Pallas kernels for 0%

commit v1 on v0

v1 whole, which is shorter than its diff:
```python
import functools

import jax
import jax.numpy as jnp
from jax import lax
from jax.experimental import pallas as pl
from jax.experimental.pallas import tpu as pltpu
from jax.sharding import PartitionSpec as P

ITERS = 4
HIGH = lax.Precision.HIGHEST
MESH = pl.DeviceIdType.MESH
F32 = jnp.float32

NXC, NYC, NZC = 4, 4, 8
GX, GY = 8, 32
PLANE = NXC * NYC


def position():
    gx, gy = lax.axis_index("gx"), lax.axis_index("gy")
    z = (gy // 8) * 2 + gx // 4
    plane = ((gy // 2) % 4) * 4 + gx % 4
    return gx, gy, z, plane, gy % 2


def device(z, plane, core):
    return ((z % 2) * 4 + plane % 4, (z // 2) * 8 + (plane // 4) * 2 + core)


def loop(low, high, body):
    def step(i, carry):
        body(i)
        return carry

    lax.fori_loop(low, high, step, 0)


def signal(sem, where):
    pl.semaphore_signal(sem, inc=1, device_id=where, device_id_type=MESH)


def greet_sum(barrier):
    _, _, z, plane, core = position()
    signal(barrier, device(z, plane, 1 - core))
    loop(1, PLANE, lambda d: signal(barrier, device(z, (plane + d) % PLANE, core)))
    loop(1, NZC, lambda d: signal(barrier, device((z + d) % NZC, plane, core)))
    return 1 + (PLANE - 1) + (NZC - 1)


def sum_scratch():
    return [
        pltpu.VMEM((2, PLANE, 24, 128), F32),
        pltpu.VMEM((PLANE, 24, 128), F32),
        pltpu.VMEM((PLANE, 24, 128), F32),
        pltpu.VMEM((NZC, 24, 128), F32),
        pltpu.SemaphoreType.DMA((2, 2)),
        pltpu.SemaphoreType.DMA((2, 2, PLANE)),
        pltpu.SemaphoreType.DMA((2, NZC)),
    ]


def all_sum(part, out, half, slots, zslots, core_sem, plane_sem, z_sem):
    _, _, z, plane, core = position()

    def core_copy(src, dst, k):
        return pltpu.make_async_remote_copy(
            src_ref=src, dst_ref=dst, send_sem=core_sem.at[k, 0], recv_sem=core_sem.at[k, 1],
            device_id=device(z, plane, 1 - core), device_id_type=MESH)

    copy = core_copy(part.at[1 - core], half, 0)
    copy.start()
    copy.wait()
    half[...] += part[core]

    def scatter(d):
        to = (plane + d) % PLANE
        return pltpu.make_async_remote_copy(
            src_ref=half.at[to], dst_ref=slots.at[d],
            send_sem=plane_sem.at[0, 0, d], recv_sem=plane_sem.at[0, 1, d],
            device_id=device(z, to, core), device_id_type=MESH)

    loop(1, PLANE, lambda d: scatter(d).start())
    loop(1, PLANE, lambda d: scatter(d).wait())
    total = half[plane]
    for d in range(1, PLANE):
        total += slots[d]
    zslots[z] = total

    def spread(d):
        return pltpu.make_async_remote_copy(
            src_ref=zslots.at[z], dst_ref=zslots.at[z],
            send_sem=z_sem.at[0, d], recv_sem=z_sem.at[1, d],
            device_id=device((z + d) % NZC, plane, core), device_id_type=MESH)

    loop(1, NZC, lambda d: spread(d).start())
    loop(1, NZC, lambda d: spread(d).wait())
    total = zslots[0]
    for k in range(1, NZC):
        total += zslots[k]
    out[core, plane] = total

    def gather(d):
        return pltpu.make_async_remote_copy(
            src_ref=out.at[core, plane], dst_ref=out.at[core, plane],
            send_sem=plane_sem.at[1, 0, d], recv_sem=plane_sem.at[1, 1, d],
            device_id=device(z, (plane + d) % PLANE, core), device_id_type=MESH)

    loop(1, PLANE, lambda d: gather(d).start())
    loop(1, PLANE, lambda d: gather(d).wait())
    copy = core_copy(out.at[core], out.at[core], 1)
    copy.start()
    copy.wait()


PAIRS = [(0, 0), (0, 1), (0, 2), (1, 1), (1, 2), (2, 2)]


def gram_blocks(rows, part):
    for k, (a, b) in enumerate(PAIRS):
        block = lax.dot_general(
            rows[128 * a:128 * a + 128, :], rows[128 * b:128 * b + 128, :],
            (((1,), (1,)), ((), ())), precision=HIGH, preferred_element_type=F32)
        flat = k * 128
        while flat < k * 128 + 128:
            inside = flat % 24
            size = min(24 - inside, k * 128 + 128 - flat)
            slab = flat // 24
            part[slab // PLANE, slab % PLANE, inside:inside + size, :] = block[flat - k * 128:flat - k * 128 + size]
            flat += size


def unpack_gram(packed):
    blocks = packed.reshape(6, 128, 128)
    u = {pair: blocks[k] for k, pair in enumerate(PAIRS)}
    return jnp.block([[u[(a, b)] if a <= b else u[(b, a)].T for b in range(3)] for a in range(3)])


def field_kernel(cells, field, gram, send, send_sem, recv_sem, *sums):
    gx, gy, _, _, _ = position()
    barrier = pltpu.get_barrier_semaphore()
    loop(1, GX, lambda d: signal(barrier, ((gx + d) % GX, gy)))
    count = greet_sum(barrier)
    pl.semaphore_wait(barrier, GX - 1 + count)

    def turn(to):
        for k in range(6):
            start = pl.multiple_of(to * 64, 64)
            pair = [cells[2 * k + h, pl.ds(start, 64), :] for h in range(2)]
            yield slice(128 * k, 128 * k + 128), jnp.concatenate(pair, axis=0).T

    def copy(d):
        to = (gx + d) % GX
        return pltpu.make_async_remote_copy(
            src_ref=send.at[to], dst_ref=field.at[gx],
            send_sem=send_sem.at[d], recv_sem=recv_sem.at[d],
            device_id=(to, gy), device_id_type=MESH)

    def push(d):
        to = (gx + d) % GX
        for lanes, block in turn(to):
            send[to, :, lanes] = block
        copy(d).start()

    loop(1, GX, push)
    for lanes, block in turn(gx):
        field[gx, :, lanes] = block
    loop(1, GX, lambda d: copy(d).wait())
    gram_blocks(field[...].reshape(384, 768), sums[0])
    all_sum(sums[0], gram, *sums[1:])


def planes_kernel(reduced, rows, gram, send, planes, send_sem, recv_sem, *sums):
    gx, gy, _, _, _ = position()
    barrier = pltpu.get_barrier_semaphore()
    loop(1, GY, lambda d: signal(barrier, (gx, (gy + d) % GY)))
    count = greet_sum(barrier)
    pl.semaphore_wait(barrier, GY - 1 + count)

    for k in range(GY):
        send[k] = reduced[3 * k:3 * k + 3, :]

    def copy(d):
        to = (gy + d) % GY
        return pltpu.make_async_remote_copy(
            src_ref=send.at[to], dst_ref=planes.at[gy],
            send_sem=send_sem.at[d], recv_sem=recv_sem.at[d],
            device_id=(gx, to), device_id_type=MESH)

    loop(1, GY, lambda d: copy(d).start())
    planes[gy] = send[gy]
    loop(1, GY, lambda d: copy(d).wait())
    for y in range(12):
        parts = [planes[:, r, 64 * y:64 * y + 64] for r in range(3)]
        parts.append(jnp.zeros((GY, 64), F32))
        for k in range(2):
            rows[k, pl.ds(y, GY, stride=12), :] = jnp.concatenate(parts[2 * k:2 * k + 2], axis=1)
    gram_blocks(jnp.concatenate([rows[0], rows[1]], axis=1), sums[0])
    all_sum(sums[0], gram, *sums[1:])


def core_kernel(part, out, send, send_sem, recv_sem):
    gx, gy, _, _, _ = position()
    home = gy // 4
    slot = gx * 4 + gy % 4
    barrier = pltpu.get_barrier_semaphore()
    loop(0, GY, lambda k: signal(barrier, (k // 4, gx * 4 + k % 4)))
    pl.semaphore_wait(barrier, GY)

    for k in range(GY):
        send[k] = part[3 * k:3 * k + 3, :]

    def copy(k):
        return pltpu.make_async_remote_copy(
            src_ref=send.at[k], dst_ref=out.at[slot],
            send_sem=send_sem.at[k], recv_sem=recv_sem.at[slot],
            device_id=(home, k), device_id_type=MESH)

    def arrival(k):
        return pltpu.make_async_remote_copy(
            src_ref=send.at[k], dst_ref=out.at[k],
            send_sem=send_sem.at[k], recv_sem=recv_sem.at[k],
            device_id=(home, k), device_id_type=MESH)

    def go(k):
        mine = (home == gx) & (k == gy)

        @pl.when(jnp.logical_not(mine))
        def _():
            copy(k).start()

        @pl.when(mine)
        def _():
            out[slot] = send[k]

    def finish(k):
        @pl.when(jnp.logical_not((home == gx) & (k == gy)))
        def _():
            copy(k).wait_send()

        @pl.when(jnp.logical_not((home == gx) & (k == slot)))
        def _():
            arrival(k).wait_recv()

    loop(0, GY, go)
    loop(0, GY, finish)


def params(number):
    return pltpu.CompilerParams(
        collective_id=number, has_side_effects=True, vmem_limit_bytes=40 * 1024 * 1024)


VM = pl.BlockSpec(memory_space=pltpu.VMEM)


def iterate(gram, start):
    own = start
    for _ in range(ITERS):
        image = jnp.dot(own, gram, precision=HIGH)
        cross = jnp.dot(image, image.T, precision=HIGH)
        lower = jnp.linalg.cholesky(cross)
        own = lax.linalg.triangular_solve(lower, image, left_side=True, lower=True)
    return own


def local(snapshot, start_x, start_y):
    gx, gy = lax.axis_index("gx"), lax.axis_index("gy")
    cells = jnp.transpose(snapshot, (1, 2, 3, 0)).reshape(12, 512, 48)
    field, gram_x = pl.pallas_call(
        field_kernel,
        out_shape=[
            jax.ShapeDtypeStruct((GX, 48, 768), F32),
            jax.ShapeDtypeStruct((2, PLANE, 24, 128), F32),
        ],
        in_specs=[VM],
        out_specs=[VM, VM],
        scratch_shapes=[
            pltpu.VMEM((GX, 48, 768), F32),
            pltpu.SemaphoreType.DMA((GX,)),
            pltpu.SemaphoreType.DMA((GX,)),
        ] + sum_scratch(),
        compiler_params=params(1),
        name="field",
    )(cells)
    basis_x = iterate(unpack_gram(gram_x), start_x.T)
    reduced = jnp.dot(basis_x, field.reshape(384, 768), precision=HIGH)
    rows, gram_y = pl.pallas_call(
        planes_kernel,
        out_shape=[
            jax.ShapeDtypeStruct((2, 384, 128), F32),
            jax.ShapeDtypeStruct((2, PLANE, 24, 128), F32),
        ],
        in_specs=[VM],
        out_specs=[VM, VM],
        scratch_shapes=[
            pltpu.VMEM((GY, 3, 768), F32),
            pltpu.VMEM((GY, 3, 768), F32),
            pltpu.SemaphoreType.DMA((GY,)),
            pltpu.SemaphoreType.DMA((GY,)),
        ] + sum_scratch(),
        compiler_params=params(2),
        name="planes",
    )(reduced)
    basis_y = iterate(unpack_gram(gram_y), start_y.T)
    core = jnp.dot(basis_y, jnp.concatenate([rows[0], rows[1, :, :64]], axis=1), precision=HIGH)
    pieces = pl.pallas_call(
        core_kernel,
        out_shape=jax.ShapeDtypeStruct((GY, 3, 192), F32),
        in_specs=[VM],
        out_specs=VM,
        scratch_shapes=[
            pltpu.VMEM((GY, 3, 192), F32),
            pltpu.SemaphoreType.DMA((GY,)),
            pltpu.SemaphoreType.DMA((GY,)),
        ],
        compiler_params=params(3),
        name="core",
    )(core)
    pieces = pieces.reshape(8, 4, 3, 3, 4, 16)
    core = jnp.transpose(pieces, (1, 3, 2, 0, 4, 5)).reshape(12, 3, 32, 16)
    own_x = lax.dynamic_slice(basis_x, (0, gx * 48), (96, 48)).T
    own_y = lax.dynamic_slice(basis_y, (0, gy * 12), (96, 12)).T
    return (own_x, own_y, core)


def solution(mesh):
    in_specs = (P("gx", "gy", None, None), P(), P())
    out_specs = (P("gx", None), P("gy", None), P("gx", "gy", None, None))
    return jax.shard_map(local, mesh=mesh, in_specs=in_specs, out_specs=out_specs, check_vma=False)
```

time: 1760 us -> 263 us (0.15)
  blocking collectives: 1020 us -> 0 us
  waiting for transfers between devices: 473 us -> 0 us
  Pallas kernels: 0 us -> 101 us
  starting transfers between devices: 40.2 us -> 0 us
  local copies, waits for them, and re-layouts: 30.9 us -> 6.62 us
  matrix products: 30 us -> 10.6 us
    psum x9 -> x0, blocking collectives: 612 us -> none  [the longest x4 484 us: iterate_y(): cross = lax.psum(jnp.dot(image.T, image, precision=HIGH), 'gy')]
    psum x1 -> x0, waiting for transfers between devices: 245 us -> none  [local(): gram_x = lax.psum(block, 'gy')]
    all_gather x6 -> x0, blocking collectives: 242 us -> none  [the longest x3 176 us: iterate_y(): full = start if step == 0 else lax.all_gather(own, 'gy', axis=0, tiled=True)]
    reduce_scatter x1 -> x0, waiting for transfers between devices: 109 us -> none  [local(): lax.psum_scatter(jnp.einsum('ys,ryc->src', chosen, cube, precision=HIGH),...]
    all_gather x1 -> x0, waiting for transfers between devices: 106 us -> none  [local(): lax.all_gather(flat, 'gx', axis=0, tiled=True)]
    pallas_call x0 -> x3, Pallas kernels: none -> 101 us  [the longest x1 46.2 us: local(): pl.pallas_call(field_kernel, out_shape=[jax.ShapeDtypeStruct((GX, 48, 768...]
    unnamed x2 -> x0, blocking collectives: 89.3 us -> none
    all_to_all x1 -> x0, blocking collectives: 75.6 us -> none  [local(): planes = lax.all_to_all(cube, 'gy', split_axis=2, concat_axis=1, tiled=True)]
  transfers between devices with their start and end apart: 13 -> 0, of which waited for: 6 -> 0; matrix products, arithmetic and copies ran while one was open for 0% -> 0% of each run, Pallas kernels for 0% -> 0%
where the time goes in v1:
time: 263 us; the launch traced here: 260 us
  other arithmetic  141 us (54%)
  Pallas kernels  101 us (38%)
  matrix products  10.6 us (4%)
  local copies, waits for them, and re-layouts  6.62 us (3%)
    another operation x24, other arithmetic, iterate(): lower = jnp.linalg.cholesky(cross)  76.3 us
    another operation x16, other arithmetic, iterate(): own = lax.linalg.triangular_solve(lower, image, left_side=True, lower=True)  64.1 us
    pallas_call x1, Pallas kernels, local(): pl.pallas_call(field_kernel, out_shape=[jax.ShapeDtypeStruct((GX, 48, 768...  46.2 us
    pallas_call x1, Pallas kernels, local(): pl.pallas_call(planes_kernel, out_shape=[jax.ShapeDtypeStruct((2, 384, 12...  39.4 us
    pallas_call x1, Pallas kernels, local(): pl.pallas_call(core_kernel, out_shape=jax.ShapeDtypeStruct((GY, 3, 192),...  15.5 us

profile of v1, /device:TPU:57, one launch (start us, length us, event | category | flops | bytes accessed | tf_op | source)
XLA Modules:
  0.0 260.4 jit_solution(9138044972827305660)
XLA Ops:
  0.7 1.9 copy-done.1
  2.6 46.2 %field.1 = (f32[8,48,768]{2,1,0:T(8,128)S(1)}, f32[2,16,24,128]{3,2,1,0:T(8,128)S(1)}) custom-call(f32[12,512,48]{2,1,0:T(8,128)S(1)} %bitcast.161), custom_call_target="tpu_custom_call" | custom-call | tf_op jit(solution)/shard_map/field/pallas_call | solution.py:270
  50.4 8.8 %cholesky.134 = f32[96,96]{1,0:T(8,128)S(1)} custom-call(f32[96,96]{1,0:T(8,128)S(1)} %fusion.37), custom_call_target="Cholesky" | custom-call | tf_op jit(solution)/shard_map/jit(cholesky)/cholesky | solution.py:262
  59.8 0.7 fusion.8
  60.5 7.4 %custom-call.12 = f32[1,96,96]{1,2,0:T(8,128)S(1)} custom-call(f32[1,96,96]{2,1,0:T(8,128)S(1)} %fusion.8), custom_call_target="InvertDiagBlocksLowerTriangular" | custom-call | tf_op jit(solution)/shard_map/triangular_solve/custom-call.0 | solution.py:263
  69.1 8.8 %cholesky.145 = f32[96,96]{1,0:T(8,128)S(1)} custom-call(f32[96,96]{1,0:T(8,128)S(1)} %fusion.35), custom_call_target="Cholesky" | custom-call | tf_op jit(solution)/shard_map/jit(cholesky)/cholesky | solution.py:262
  78.6 0.7 fusion.9
  79.3 7.4 %custom-call.13 = f32[1,96,96]{1,2,0:T(8,128)S(1)} custom-call(f32[1,96,96]{2,1,0:T(8,128)S(1)} %fusion.9), custom_call_target="InvertDiagBlocksLowerTriangular" | custom-call | tf_op jit(solution)/shard_map/triangular_solve/custom-call.0 | solution.py:263
  87.9 9.3 %cholesky.156 = f32[96,96]{1,0:T(8,128)S(1)} custom-call(f32[96,96]{1,0:T(8,128)S(1)} %fusion.32), custom_call_target="Cholesky" | custom-call | tf_op jit(solution)/shard_map/jit(cholesky)/cholesky | solution.py:262
  97.9 0.7 fusion.10
  98.5 7.4 %custom-call.14 = f32[1,96,96]{1,2,0:T(8,128)S(1)} custom-call(f32[1,96,96]{2,1,0:T(8,128)S(1)} %fusion.10), custom_call_target="InvertDiagBlocksLowerTriangular" | custom-call | tf_op jit(solution)/shard_map/triangular_solve/custom-call.0 | solution.py:263
  107.2 8.8 %cholesky.167 = f32[96,96]{1,0:T(8,128)S(1)} custom-call(f32[96,96]{1,0:T(8,128)S(1)} %fusion.29), custom_call_target="Cholesky" | custom-call | tf_op jit(solution)/shard_map/jit(cholesky)/cholesky | solution.py:262
  116.6 0.7 fusion.11
  117.3 7.4 %custom-call.15 = f32[1,96,96]{1,2,0:T(8,128)S(1)} custom-call(f32[1,96,96]{2,1,0:T(8,128)S(1)} %fusion.11), custom_call_target="InvertDiagBlocksLowerTriangular" | custom-call | tf_op jit(solution)/shard_map/triangular_solve/custom-call.0 | solution.py:263
  125.0 0.8 fusion.59.reduced
  125.9 39.4 %planes.1 = (f32[2,384,128]{2,1,0:T(8,128)S(1)}, f32[2,16,24,128]{3,2,1,0:T(8,128)S(1)}) custom-call(f32[96,768]{1,0:T(8,128)S(1)} %fusion.59.reduced), custom_call_target="tpu_custom_call" | custom-call | tf_op jit(solution)/shard_map/planes/pallas_call | solution.py:288
  166.9 8.8 %cholesky.178 = f32[96,96]{1,0:T(8,128)S(1)} custom-call(f32[96,96]{1,0:T(8,128)S(1)} %fusion.26), custom_call_target="Cholesky" | custom-call | tf_op jit(solution)/shard_map/jit(cholesky)/cholesky | solution.py:262
  176.4 0.7 fusion.12
  177.0 7.4 %custom-call.16 = f32[1,96,96]{1,2,0:T(8,128)S(1)} custom-call(f32[1,96,96]{2,1,0:T(8,128)S(1)} %fusion.12), custom_call_target="InvertDiagBlocksLowerTriangular" | custom-call | tf_op jit(solution)/shard_map/triangular_solve/custom-call.0 | solution.py:263
  185.7 8.8 %cholesky.189 = f32[96,96]{1,0:T(8,128)S(1)} custom-call(f32[96,96]{1,0:T(8,128)S(1)} %fusion.24), custom_call_target="Cholesky" | custom-call | tf_op jit(solution)/shard_map/jit(cholesky)/cholesky | solution.py:262
  195.1 0.7 fusion.13
  195.8 7.4 %custom-call.17 = f32[1,96,96]{1,2,0:T(8,128)S(1)} custom-call(f32[1,96,96]{2,1,0:T(8,128)S(1)} %fusion.13), custom_call_target="InvertDiagBlocksLowerTriangular" | custom-call | tf_op jit(solution)/shard_map/triangular_solve/custom-call.0 | solution.py:263
  204.4 9.0 %cholesky.200 = f32[96,96]{1,0:T(8,128)S(1)} custom-call(f32[96,96]{1,0:T(8,128)S(1)} %fusion.21), custom_call_target="Cholesky" | custom-call | tf_op jit(solution)/shard_map/jit(cholesky)/cholesky | solution.py:262
  214.1 0.7 fusion.14
  214.8 7.4 %custom-call.18 = f32[1,96,96]{1,2,0:T(8,128)S(1)} custom-call(f32[1,96,96]{2,1,0:T(8,128)S(1)} %fusion.14), custom_call_target="InvertDiagBlocksLowerTriangular" | custom-call | tf_op jit(solution)/shard_map/triangular_solve/custom-call.0 | solution.py:263
  223.4 8.8 %cholesky.211 = f32[96,96]{1,0:T(8,128)S(1)} custom-call(f32[96,96]{1,0:T(8,128)S(1)} %fusion.18), custom_call_target="Cholesky" | custom-call | tf_op jit(solution)/shard_map/jit(cholesky)/cholesky | solution.py:262
  232.9 0.7 fusion.15
  233.5 7.4 %custom-call.19 = f32[1,96,96]{1,2,0:T(8,128)S(1)} custom-call(f32[1,96,96]{2,1,0:T(8,128)S(1)} %fusion.15), custom_call_target="InvertDiagBlocksLowerTriangular" | custom-call | tf_op jit(solution)/shard_map/triangular_solve/custom-call.0 | solution.py:263
  241.7 15.5 %core.1 = f32[32,3,192]{2,1,0:T(4,128)S(1)} custom-call(f32[96,192]{1,0:T(8,128)S(1)} %fusion.part), custom_call_target="tpu_custom_call" | custom-call | tf_op jit(solution)/shard_map/core/pallas_call | solution.py:307
  257.7 0.9 copy.49
  258.7 0.7 copy.48
  259.5 0.7 copy.47
  (83 shorter events, 17.6 us)
Async XLA Ops:
  0.6 48.8 %copy-start = (f32[384,96]{0,1:T(8,128)S(1)}, f32[384,96]{0,1:T(8,128)}, u32[]{:S(2)}) copy-start(f32[384,96]{0,1:T(8,128)} %param.7) | copy-start | bytes 442372
  0.6 1.9 copy-start.1
  125.9 40.1 %copy-start.2 = (f32[384,96]{0,1:T(8,128)S(1)}, f32[384,96]{0,1:T(8,128)}, u32[]{:S(2)}) copy-start(f32[384,96]{0,1:T(8,128)} %param.8) | copy-start | bytes 442372

commit v2 on v1

--- a/solution.py
+++ b/solution.py
@@ -11,6 +11,7 @@
 HIGH = lax.Precision.HIGHEST
 MESH = pl.DeviceIdType.MESH
 F32 = jnp.float32
+BF16 = jnp.bfloat16
 
 NXC, NYC, NZC = 4, 4, 8
 GX, GY = 8, 32
@@ -130,12 +131,6 @@
             flat += size
 
 
-def unpack_gram(packed):
-    blocks = packed.reshape(6, 128, 128)
-    u = {pair: blocks[k] for k, pair in enumerate(PAIRS)}
-    return jnp.block([[u[(a, b)] if a <= b else u[(b, a)].T for b in range(3)] for a in range(3)])
-
-
 def field_kernel(cells, field, gram, send, send_sem, recv_sem, *sums):
     gx, gy, _, _, _ = position()
     barrier = pltpu.get_barrier_semaphore()
@@ -208,7 +203,7 @@
     pl.semaphore_wait(barrier, GY)
 
     for k in range(GY):
-        send[k] = part[3 * k:3 * k + 3, :]
+        send[k] = part[3 * k:3 * k + 3, :192]
 
     def copy(k):
         return pltpu.make_async_remote_copy(
@@ -254,18 +249,122 @@
 VM = pl.BlockSpec(memory_space=pltpu.VMEM)
 
 
+def split(a):
+    hi = a.astype(BF16)
+    rest = a - hi.astype(F32)
+    mid = rest.astype(BF16)
+    return hi, mid, (rest - mid.astype(F32)).astype(BF16)
+
+
+def dot(a, b, turned=False):
+    dims = (((1,), (1 if turned else 0,)), ((), ()))
+
+    def term(i, j):
+        return lax.dot_general(a[i], b[j], dims, preferred_element_type=F32)
+
+    small = term(0, 2) + term(2, 0) + term(1, 1)
+    return term(0, 0) + (term(0, 1) + term(1, 0) + small)
+
+
+def inverse_factor(cross, panel=16):
+    rank = cross.shape[0]
+    rows = lax.broadcasted_iota(jnp.int32, (panel, 128), 0)
+    left = cross
+    right = (lax.broadcasted_iota(jnp.int32, (rank, 128), 0)
+             == lax.broadcasted_iota(jnp.int32, (rank, 128), 1)).astype(F32)
+    outs = []
+    for first in range(0, rank, panel):
+        solved_left, solved_right, lower = left[:panel], right[:panel], right[:panel]
+        columns = [
+            jnp.broadcast_to(left[:panel, first + j:first + j + 1], (panel, 128)) for j in range(panel)]
+        inverse = jnp.zeros((panel, 128), F32)
+        for k in range(panel):
+            pivot = 1.0 / jnp.broadcast_to(columns[k][k:k + 1], (panel, 128))
+            ratio = columns[k] * pivot
+            others = jnp.where(rows == k, 0.0, ratio)
+            below = jnp.where(rows > k, ratio, 0.0)
+            inverse = jnp.where(rows == k, pivot, inverse)
+            for j in range(k + 1, panel):
+                columns[j] = columns[j] - others * columns[j][k:k + 1]
+            solved_left = solved_left - others * solved_left[k:k + 1]
+            solved_right = solved_right - others * solved_right[k:k + 1]
+            lower = lower - below * lower[k:k + 1]
+        outs.append(lower * jnp.sqrt(inverse))
+        if first + panel == rank:
+            break
+        solved = jnp.concatenate([solved_left * inverse, solved_right * inverse], axis=1)
+
+        def place(block):
+            parts = [block, jnp.zeros((128 - first - panel, 256), BF16)]
+            if first:
+                parts = [jnp.zeros((first, 256), BF16)] + parts
+            return jnp.concatenate(parts, axis=0)
+
+        high, mid, low = (place(t) for t in split(solved))
+        a_high, a_mid, a_low = split(left[panel:])
+
+        def wide(a, b, c, d):
+            return jnp.dot(
+                jnp.concatenate([a, b], axis=1), jnp.concatenate([c, d], axis=0),
+                preferred_element_type=F32)
+
+        update = wide(a_high, a_mid, high, high) + (
+            wide(a_high, a_mid, mid, mid) + wide(a_high, a_low, low, high))
+        left = left[panel:] - update[:, :128]
+        right = right[panel:] - update[:, 128:]
+    return jnp.concatenate(outs, axis=0)
+
+
 def iterate(gram, start):
+    blocks = gram.reshape(6, 128, 128)
+    upper = {pair: blocks[k] for k, pair in enumerate(PAIRS)}
+    full = jnp.concatenate([
+        jnp.concatenate([upper[(a, b)] if a <= b else upper[(b, a)].T for b in range(3)], axis=1)
+        for a in range(3)], axis=0)
+    gram = split(full)
     own = start
     for _ in range(ITERS):
-        image = jnp.dot(own, gram, precision=HIGH)
-        cross = jnp.dot(image, image.T, precision=HIGH)
-        lower = jnp.linalg.cholesky(cross)
-        own = lax.linalg.triangular_solve(lower, image, left_side=True, lower=True)
+        image = dot(split(own), gram)
+        image = jnp.concatenate([image, jnp.zeros((32, 384), F32)], axis=0)
+        parts = split(image)
+        cross = dot([t[:96] for t in parts], parts, turned=True)
+        own = dot(split(inverse_factor(cross)), parts)
     return own
 
 
+def own_rows(parts, first, count):
+    row = lax.broadcasted_iota(jnp.int32, (count, 384), 0)
+    pick = (lax.broadcasted_iota(jnp.int32, (count, 384), 1) == row + first).astype(BF16)
+    dims = (((1,), (1,)), ((), ()))
+    high, mid, low = (
+        lax.dot_general(pick, t, dims, preferred_element_type=F32) for t in parts)
+    return high + mid + low
+
+
+def basis_x_kernel(gram, start, field, own, reduced):
+    parts = split(iterate(gram[...], start[...]))
+    own[...] = own_rows(parts, lax.axis_index("gx") * 48, 48)
+    reduced[...] = dot(parts, split(field[...].reshape(384, 768)))
+
+
+def basis_y_kernel(gram, start, rows, own, core):
+    parts = split(iterate(gram[...], start[...]))
+    own[...] = own_rows(parts, lax.axis_index("gy") * 12, 12)
+    core[...] = dot(parts, split(jnp.concatenate([rows[0], rows[1]], axis=1)))
+
+
+def compute(body, out, name):
+    return pl.pallas_call(
+        body,
+        out_shape=[jax.ShapeDtypeStruct(shape, F32) for shape in out],
+        in_specs=[VM] * 3,
+        out_specs=[VM] * 2,
+        compiler_params=pltpu.CompilerParams(vmem_limit_bytes=40 * 1024 * 1024),
+        name=name,
+    )
+
+
 def local(snapshot, start_x, start_y):
-    gx, gy = lax.axis_index("gx"), lax.axis_index("gy")
     cells = jnp.transpose(snapshot, (1, 2, 3, 0)).reshape(12, 512, 48)
     field, gram_x = pl.pallas_call(
         field_kernel,
@@ -283,8 +382,7 @@
         compiler_params=params(1),
         name="field",
     )(cells)
-    basis_x = iterate(unpack_gram(gram_x), start_x.T)
-    reduced = jnp.dot(basis_x, field.reshape(384, 768), precision=HIGH)
+    own_x, reduced = compute(basis_x_kernel, [(48, 96), (96, 768)], "basis_x")(gram_x, start_x.T, field)
     rows, gram_y = pl.pallas_call(
         planes_kernel,
         out_shape=[
@@ -302,8 +400,7 @@
         compiler_params=params(2),
         name="planes",
     )(reduced)
-    basis_y = iterate(unpack_gram(gram_y), start_y.T)
-    core = jnp.dot(basis_y, jnp.concatenate([rows[0], rows[1, :, :64]], axis=1), precision=HIGH)
+    own_y, core = compute(basis_y_kernel, [(12, 96), (96, 256)], "basis_y")(gram_y, start_y.T, rows)
     pieces = pl.pallas_call(
         core_kernel,
         out_shape=jax.ShapeDtypeStruct((GY, 3, 192), F32),
@@ -319,8 +416,6 @@
     )(core)
     pieces = pieces.reshape(8, 4, 3, 3, 4, 16)
     core = jnp.transpose(pieces, (1, 3, 2, 0, 4, 5)).reshape(12, 3, 32, 16)
-    own_x = lax.dynamic_slice(basis_x, (0, gx * 48), (96, 48)).T
-    own_y = lax.dynamic_slice(basis_y, (0, gy * 12), (96, 12)).T
     return (own_x, own_y, core)
 
 

time: 263 us -> 139 us (0.53)
  other arithmetic: 141 us -> 0 us
  Pallas kernels: 101 us -> 135 us
  matrix products: 10.6 us -> 0 us
  local copies, waits for them, and re-layouts: 6.62 us -> 3.31 us
    another operation x40 -> x0, other arithmetic: 140 us -> none  [the longest x24 76.3 us: iterate(): lower = jnp.linalg.cholesky(cross)]
    pallas_call x0 -> x2, Pallas kernels: none -> 34 us  [the longest x1 17.1 us: local(): compute(basis_x_kernel, [(48, 96), (96, 768)], 'basis_x')]
    dot_general x18 -> x0, matrix products: 7.93 us -> none  [the longest x8 4.1 us: iterate(): image = jnp.dot(own, gram, precision=HIGH)]
    another operation x8 -> x0, matrix products: 2.64 us -> none  [iterate(): own = lax.linalg.triangular_solve(lower, image, left_side=True, lower=True)]
where the time goes in v2:
time: 139 us
  Pallas kernels  135 us (97%)
  local copies, waits for them, and re-layouts  3.31 us (2%)
    pallas_call x1, Pallas kernels, local(): pl.pallas_call(field_kernel, out_shape=[jax.ShapeDtypeStruct((GX, 48, 768...  46.3 us
    pallas_call x1, Pallas kernels, local(): pl.pallas_call(planes_kernel, out_shape=[jax.ShapeDtypeStruct((2, 384, 12...  39.4 us
    pallas_call x1, Pallas kernels, local(): compute(basis_x_kernel, [(48, 96), (96, 768)], 'basis_x')  17.1 us
    pallas_call x1, Pallas kernels, local(): compute(basis_y_kernel, [(12, 96), (96, 256)], 'basis_y')  16.9 us
    pallas_call x1, Pallas kernels, local(): pl.pallas_call(core_kernel, out_shape=jax.ShapeDtypeStruct((GY, 3, 192),...  15.3 us
    unnamed x7, local copies, waits for them, and re-layouts  2.82 us

profile of v2, /device:TPU:57, one launch (start us, length us, event | category | flops | bytes accessed | tf_op | source)
XLA Modules:
  0.0 139.0 jit_solution(12753487813389303071)
XLA Ops:
  0.6 0.0 copy-start
  0.6 1.9 %copy-done = f32[48,12,32,16]{0,3,2,1:T(8,128)S(1)} copy-done((f32[48,12,32,16]{0,3,2,1:T(8,128)S(1)}, f32[48,12,32,16]{0,3,2,1:T(8,128)}, u32[]{:S(2)}) %copy-start) | copy-done | bytes 1179672
  2.5 0.0 copy-start.2
  2.5 0.0 copy-start.1
  2.5 46.3 %field.1 = (f32[8,48,768]{2,1,0:T(8,128)S(1)}, f32[2,16,24,128]{3,2,1,0:T(8,128)S(1)}) custom-call(f32[12,512,48]{2,1,0:T(8,128)S(1)} %bitcast.9), custom_call_target="tpu_custom_call" | custom-call | tf_op jit(solution)/shard_map/field/pallas_call | solution.py:369
  48.9 0.0 copy-done.2
  48.9 17.1 %basis_x.1 = (f32[48,96]{1,0:T(8,128)}, f32[96,768]{1,0:T(8,128)S(1)}) custom-call(f32[2,16,24,128]{3,2,1,0:T(8,128)S(1)} %get-tuple-element.11.gram, f32[96,384]{1,0:T(8,128)S(1)} %bitcast.11, f32[8,48,768]{2,1,0:T(8,128)S(1)} %get-tuple-element.12.field), custom_call_target="tpu_custom_call" | custom-call | tf_op jit(solution)/shard_map/basis_x/pallas_call | solution.py:385
  66.0 39.4 %planes.1 = (f32[2,384,128]{2,1,0:T(8,128)S(1)}, f32[2,16,24,128]{3,2,1,0:T(8,128)S(1)}) custom-call(f32[96,768]{1,0:T(8,128)S(1)} %get-tuple-element.14.reduced), custom_call_target="tpu_custom_call" | custom-call | tf_op jit(solution)/shard_map/planes/pallas_call | solution.py:386
  105.4 0.0 copy-done.1
  105.4 16.9 %basis_y.1 = (f32[12,96]{1,0:T(8,128)}, f32[96,256]{1,0:T(8,128)S(1)}) custom-call(f32[2,16,24,128]{3,2,1,0:T(8,128)S(1)} %get-tuple-element.15.gram, f32[96,384]{1,0:T(8,128)S(1)} %bitcast.10, f32[2,384,128]{2,1,0:T(8,128)S(1)} %get-tuple-element.16.rows), custom_call_target="tpu_custom_call" | custom-call | tf_op jit(solution)/shard_map/basis_y/pallas_call | solution.py:403
  122.3 15.3 %core.1 = f32[32,3,192]{2,1,0:T(4,128)S(1)} custom-call(f32[96,256]{1,0:T(8,128)S(1)} %get-tuple-element.18.part), custom_call_target="tpu_custom_call" | custom-call | tf_op jit(solution)/shard_map/core/pallas_call | solution.py:404
  137.6 0.3 reshape.16
  137.9 0.2 copy.8
  138.1 0.9 copy.9
  (1 shorter events, 0.0 us)
Async XLA Ops:
  0.6 1.9 %copy-start = (f32[48,12,32,16]{0,3,2,1:T(8,128)S(1)}, f32[48,12,32,16]{0,3,2,1:T(8,128)}, u32[]{:S(2)}) copy-start(f32[48,12,32,16]{0,3,2,1:T(8,128)} %param.3) | copy-start | bytes 3538948
  2.5 46.4 %copy-start.2 = (f32[384,96]{0,1:T(8,128)S(1)}, f32[384,96]{0,1:T(8,128)}, u32[]{:S(2)}) copy-start(f32[384,96]{0,1:T(8,128)} %param.4) | copy-start | bytes 442372
  2.5 102.8 %copy-start.1 = (f32[384,96]{0,1:T(8,128)S(1)}, f32[384,96]{0,1:T(8,128)}, u32[]{:S(2)}) copy-start(f32[384,96]{0,1:T(8,128)} %param.5) | copy-start | bytes 442372

commit v3 on v1

v3 whole, which is shorter than its diff:
```python
import jax
import jax.numpy as jnp
from jax import lax
from jax.experimental import pallas as pl
from jax.experimental.pallas import tpu as pltpu
from jax.sharding import PartitionSpec as P

ITERS = 4
HIGH = lax.Precision.HIGHEST
MESH = pl.DeviceIdType.MESH
F32 = jnp.float32
BF16 = jnp.bfloat16

NXC, NYC, NZC = 4, 4, 8
GX, GY = 8, 32
PLANE = NXC * NYC


def position():
    gx, gy = lax.axis_index("gx"), lax.axis_index("gy")
    z = (gy // 8) * 2 + gx // 4
    plane = ((gy // 2) % 4) * 4 + gx % 4
    return gx, gy, z, plane, gy % 2


def device(z, plane, core):
    return ((z % 2) * 4 + plane % 4, (z // 2) * 8 + (plane // 4) * 2 + core)


def loop(low, high, body):
    def step(i, carry):
        body(i)
        return carry

    lax.fori_loop(low, high, step, 0)


def signal(sem, where):
    pl.semaphore_signal(sem, inc=1, device_id=where, device_id_type=MESH)


def sum_scratch():
    return [
        pltpu.VMEM((2, PLANE, 24, 128), F32),
        pltpu.VMEM((2, PLANE, 24, 128), F32),
        pltpu.VMEM((PLANE, 24, 128), F32),
        pltpu.VMEM((PLANE, 24, 128), F32),
        pltpu.VMEM((NZC, 24, 128), F32),
        pltpu.SemaphoreType.DMA((2, 2)),
        pltpu.SemaphoreType.DMA((2, 2, PLANE)),
        pltpu.SemaphoreType.DMA((2, NZC)),
    ]


def all_sum(part, out, half, slots, zslots, core_sem, plane_sem, z_sem):
    _, _, z, plane, core = position()

    def core_copy(src, dst, k):
        return pltpu.make_async_remote_copy(
            src_ref=src, dst_ref=dst, send_sem=core_sem.at[k, 0], recv_sem=core_sem.at[k, 1],
            device_id=device(z, plane, 1 - core), device_id_type=MESH)

    copy = core_copy(part.at[1 - core], half, 0)
    copy.start()
    copy.wait()
    half[...] += part[core]

    def scatter(d):
        to = (plane + d) % PLANE
        return pltpu.make_async_remote_copy(
            src_ref=half.at[to], dst_ref=slots.at[d],
            send_sem=plane_sem.at[0, 0, d], recv_sem=plane_sem.at[0, 1, d],
            device_id=device(z, to, core), device_id_type=MESH)

    loop(1, PLANE, lambda d: scatter(d).start())
    loop(1, PLANE, lambda d: scatter(d).wait())
    total = half[plane]
    for d in range(1, PLANE):
        total += slots[d]
    zslots[z] = total

    def spread(d):
        return pltpu.make_async_remote_copy(
            src_ref=zslots.at[z], dst_ref=zslots.at[z],
            send_sem=z_sem.at[0, d], recv_sem=z_sem.at[1, d],
            device_id=device((z + d) % NZC, plane, core), device_id_type=MESH)

    loop(1, NZC, lambda d: spread(d).start())
    loop(1, NZC, lambda d: spread(d).wait())
    total = zslots[0]
    for k in range(1, NZC):
        total += zslots[k]
    out[core, plane] = total

    def gather(d):
        return pltpu.make_async_remote_copy(
            src_ref=out.at[core, plane], dst_ref=out.at[core, plane],
            send_sem=plane_sem.at[1, 0, d], recv_sem=plane_sem.at[1, 1, d],
            device_id=device(z, (plane + d) % PLANE, core), device_id_type=MESH)

    loop(1, PLANE, lambda d: gather(d).start())
    loop(1, PLANE, lambda d: gather(d).wait())
    copy = core_copy(out.at[core], out.at[core], 1)
    copy.start()
    copy.wait()


PAIRS = [(0, 0), (0, 1), (0, 2), (1, 1), (1, 2), (2, 2)]


def gram_blocks(rows, part):
    for k, (a, b) in enumerate(PAIRS):
        block = lax.dot_general(
            rows[128 * a:128 * a + 128, :], rows[128 * b:128 * b + 128, :],
            (((1,), (1,)), ((), ())), precision=HIGH, preferred_element_type=F32)
        flat = k * 128
        while flat < k * 128 + 128:
            inside = flat % 24
            size = min(24 - inside, k * 128 + 128 - flat)
            slab = flat // 24
            part[slab // PLANE, slab % PLANE, inside:inside + size, :] = block[flat - k * 128:flat - k * 128 + size]
            flat += size


def split(a):
    hi = a.astype(BF16)
    rest = a - hi.astype(F32)
    mid = rest.astype(BF16)
    return hi, mid, (rest - mid.astype(F32)).astype(BF16)


def dot(a, b, turned=False):
    dims = (((1,), (1 if turned else 0,)), ((), ()))

    def term(i, j):
        return lax.dot_general(a[i], b[j], dims, preferred_element_type=F32)

    small = term(0, 2) + term(2, 0) + term(1, 1)
    return term(0, 0) + (term(0, 1) + term(1, 0) + small)


def inverse_factor(cross, panel=16):
    rank = cross.shape[0]
    rows = lax.broadcasted_iota(jnp.int32, (panel, 128), 0)
    left = cross
    right = (lax.broadcasted_iota(jnp.int32, (rank, 128), 0)
             == lax.broadcasted_iota(jnp.int32, (rank, 128), 1)).astype(F32)
    outs = []
    for first in range(0, rank, panel):
        solved_left, solved_right, lower = left[:panel], right[:panel], right[:panel]
        columns = [
            jnp.broadcast_to(left[:panel, first + j:first + j + 1], (panel, 128)) for j in range(panel)]
        inverse = jnp.zeros((panel, 128), F32)
        for k in range(panel):
            pivot = 1.0 / jnp.broadcast_to(columns[k][k:k + 1], (panel, 128))
            ratio = columns[k] * pivot
            others = jnp.where(rows == k, 0.0, ratio)
            below = jnp.where(rows > k, ratio, 0.0)
            inverse = jnp.where(rows == k, pivot, inverse)
            for j in range(k + 1, panel):
                columns[j] = columns[j] - others * columns[j][k:k + 1]
            solved_left = solved_left - others * solved_left[k:k + 1]
            solved_right = solved_right - others * solved_right[k:k + 1]
            lower = lower - below * lower[k:k + 1]
        outs.append(lower * jnp.sqrt(inverse))
        if first + panel == rank:
            break
        solved = jnp.concatenate([solved_left * inverse, solved_right * inverse], axis=1)

        def place(block):
            parts = [block, jnp.zeros((128 - first - panel, 256), BF16)]
            if first:
                parts = [jnp.zeros((first, 256), BF16)] + parts
            return jnp.concatenate(parts, axis=0)

        high, mid, low = (place(t) for t in split(solved))
        a_high, a_mid, a_low = split(left[panel:])

        def wide(a, b, c, d):
            return jnp.dot(
                jnp.concatenate([a, b], axis=1), jnp.concatenate([c, d], axis=0),
                preferred_element_type=F32)

        update = wide(a_high, a_mid, high, high) + (
            wide(a_high, a_mid, mid, mid) + wide(a_high, a_low, low, high))
        left = left[panel:] - update[:, :128]
        right = right[panel:] - update[:, 128:]
    return jnp.concatenate(outs, axis=0)


def iterate(packed, start, gram, own):
    blocks = packed[...].reshape(6, 128, 128)
    upper = {pair: blocks[k] for k, pair in enumerate(PAIRS)}
    full = jnp.concatenate([
        jnp.concatenate([upper[(a, b)] if a <= b else upper[(b, a)].T for b in range(3)], axis=1)
        for a in range(3)], axis=0)
    for k, term in enumerate(split(full)):
        gram[k] = term
    own[...] = start[...]

    def step(_):
        image = dot(split(own[...]), [gram[k] for k in range(3)])
        image = jnp.concatenate([image, jnp.zeros((32, 384), F32)], axis=0)
        parts = split(image)
        cross = dot([t[:96] for t in parts], parts, turned=True)
        own[...] = dot(split(inverse_factor(cross)), parts)

    loop(0, ITERS, step)


def own_rows(parts, first, count):
    row = lax.broadcasted_iota(jnp.int32, (count, 384), 0)
    pick = (lax.broadcasted_iota(jnp.int32, (count, 384), 1) == row + first).astype(BF16)
    dims = (((1,), (1,)), ((), ()))
    high, mid, low = (
        lax.dot_general(pick, t, dims, preferred_element_type=F32) for t in parts)
    return high + mid + low


def greet(barrier):
    gx, gy, z, plane, core = position()
    loop(1, GX, lambda d: signal(barrier, ((gx + d) % GX, gy)))
    signal(barrier, device(z, plane, 1 - core))
    loop(1, PLANE, lambda d: signal(barrier, device(z, (plane + d) % PLANE, core)))
    loop(1, NZC, lambda d: signal(barrier, device((z + d) % NZC, plane, core)))
    loop(1, GY, lambda d: signal(barrier, (gx, (gy + d) % GY)))
    loop(0, GY, lambda k: signal(barrier, (k // 4, gx * 4 + k % 4)))
    return GX - 1 + 1 + PLANE - 1 + NZC - 1 + GY - 1 + GY


def window_kernel(cells, start_x, start_y, own_x, own_y, out, send_x, field, send_y, planes, rows, send_c,
                  basis, gram, sem_x, sem_y, sem_c, *sums):
    gx, gy, _, _, _ = position()
    sums_x, sums_y = sums[:len(sums) // 2], sums[len(sums) // 2:]
    barrier = pltpu.get_barrier_semaphore()
    count = greet(barrier)

    def turn(to):
        for k in range(6):
            start = pl.multiple_of(to * 64, 64)
            pair = [cells[2 * k + h, pl.ds(start, 64), :] for h in range(2)]
            yield slice(128 * k, 128 * k + 128), jnp.concatenate(pair, axis=0).T

    def push_x(d):
        to = (gx + d) % GX
        for lanes, block in turn(to):
            send_x[to, :, lanes] = block

    def copy_x(d):
        to = (gx + d) % GX
        return pltpu.make_async_remote_copy(
            src_ref=send_x.at[to], dst_ref=field.at[gx],
            send_sem=sem_x.at[0, d], recv_sem=sem_x.at[1, d],
            device_id=(to, gy), device_id_type=MESH)

    loop(1, GX, push_x)
    for lanes, block in turn(gx):
        field[gx, :, lanes] = block
    pl.semaphore_wait(barrier, count)
    loop(1, GX, lambda d: copy_x(d).start())
    loop(1, GX, lambda d: copy_x(d).wait())
    gram_blocks(field[...].reshape(384, 768), sums_x[0])
    all_sum(*sums_x)
    iterate(sums_x[1], start_x, gram, basis)
    parts = split(basis[...])
    own_x[...] = own_rows(parts, gx * 48, 48)

    reduced = dot(parts, split(field[...].reshape(384, 768)))
    for k in range(GY):
        send_y[k] = reduced[3 * k:3 * k + 3, :]

    def copy_y(d):
        to = (gy + d) % GY
        return pltpu.make_async_remote_copy(
            src_ref=send_y.at[to], dst_ref=planes.at[gy],
            send_sem=sem_y.at[0, d], recv_sem=sem_y.at[1, d],
            device_id=(gx, to), device_id_type=MESH)

    loop(1, GY, lambda d: copy_y(d).start())
    planes[gy] = send_y[gy]
    loop(1, GY, lambda d: copy_y(d).wait())
    for y in range(12):
        pieces = [planes[:, r, 64 * y:64 * y + 64] for r in range(3)]
        pieces.append(jnp.zeros((GY, 64), F32))
        for k in range(2):
            rows[k, pl.ds(y, GY, stride=12), :] = jnp.concatenate(pieces[2 * k:2 * k + 2], axis=1)
    gram_blocks(jnp.concatenate([rows[0], rows[1]], axis=1), sums_y[0])
    all_sum(*sums_y)
    iterate(sums_y[1], start_y, gram, basis)
    parts = split(basis[...])
    own_y[...] = own_rows(parts, gy * 12, 12)

    core = dot(parts, split(jnp.concatenate([rows[0], rows[1]], axis=1)))
    for k in range(GY):
        send_c[k] = core[3 * k:3 * k + 3, :192]
    home = gy // 4
    slot = gx * 4 + gy % 4

    def copy_c(k, to):
        return pltpu.make_async_remote_copy(
            src_ref=send_c.at[k], dst_ref=out.at[to],
            send_sem=sem_c.at[0, k], recv_sem=sem_c.at[1, to],
            device_id=(home, k), device_id_type=MESH)

    def go(k):
        mine = (home == gx) & (k == gy)

        @pl.when(jnp.logical_not(mine))
        def _():
            copy_c(k, slot).start()

        @pl.when(mine)
        def _():
            out[slot] = send_c[k]

    def finish(k):
        @pl.when(jnp.logical_not((home == gx) & (k == gy)))
        def _():
            copy_c(k, slot).wait_send()

        @pl.when(jnp.logical_not((home == gx) & (k == slot)))
        def _():
            copy_c(k, k).wait_recv()

    loop(0, GY, go)
    loop(0, GY, finish)


VM = pl.BlockSpec(memory_space=pltpu.VMEM)


def local(snapshot, start_x, start_y):
    cells = jnp.transpose(snapshot, (1, 2, 3, 0)).reshape(12, 512, 48)
    own_x, own_y, pieces = pl.pallas_call(
        window_kernel,
        out_shape=[jax.ShapeDtypeStruct(shape, F32) for shape in ((48, 96), (12, 96), (GY, 3, 192))],
        in_specs=[VM] * 3,
        out_specs=[VM] * 3,
        scratch_shapes=[
            pltpu.VMEM((GX, 48, 768), F32),
            pltpu.VMEM((GX, 48, 768), F32),
            pltpu.VMEM((GY, 3, 768), F32),
            pltpu.VMEM((GY, 3, 768), F32),
            pltpu.VMEM((2, 384, 128), F32),
            pltpu.VMEM((GY, 3, 192), F32),
            pltpu.VMEM((96, 384), F32),
            pltpu.VMEM((3, 384, 384), BF16),
            pltpu.SemaphoreType.DMA((2, GX)),
            pltpu.SemaphoreType.DMA((2, GY)),
            pltpu.SemaphoreType.DMA((2, GY)),
        ] + sum_scratch() + sum_scratch(),
        compiler_params=pltpu.CompilerParams(
            collective_id=1, has_side_effects=True, vmem_limit_bytes=48 * 1024 * 1024),
        name="window",
    )(cells, start_x.T, start_y.T)
    pieces = pieces.reshape(8, 4, 3, 3, 4, 16)
    core = jnp.transpose(pieces, (1, 3, 2, 0, 4, 5)).reshape(12, 3, 32, 16)
    return (own_x, own_y, core)


def solution(mesh):
    in_specs = (P("gx", "gy", None, None), P(), P())
    out_specs = (P("gx", None), P("gy", None), P("gx", "gy", None, None))
    return jax.shard_map(local, mesh=mesh, in_specs=in_specs, out_specs=out_specs, check_vma=False)
```

time: 263 us -> 134 us (0.51)
  other arithmetic: 141 us -> 0 us
  Pallas kernels: 101 us -> 126 us
  matrix products: 10.6 us -> 0 us
    another operation x40 -> x0, other arithmetic: 140 us -> none  [the longest x24 76.3 us: iterate(): lower = jnp.linalg.cholesky(cross)]
    pallas_call x3 -> x1, Pallas kernels: 101 us -> 126 us  [local(): pl.pallas_call(window_kernel, out_shape=[jax.ShapeDtypeStruct(shape, F32)...]
    dot_general x18 -> x0, matrix products: 7.93 us -> none  [the longest x8 4.1 us: iterate(): image = jnp.dot(own, gram, precision=HIGH)]
    another operation x8 -> x0, matrix products: 2.64 us -> none  [iterate(): own = lax.linalg.triangular_solve(lower, image, left_side=True, lower=True)]
    unnamed x15 -> x9, local copies, waits for them, and re-layouts: 4.78 us -> 5.84 us
where the time goes in v3:
time: 134 us; the launch traced here: 133 us
  Pallas kernels  126 us (94%)
  local copies, waits for them, and re-layouts  6.33 us (5%)
    pallas_call x1, Pallas kernels, local(): pl.pallas_call(window_kernel, out_shape=[jax.ShapeDtypeStruct(shape, F32)...  126 us
    unnamed x9, local copies, waits for them, and re-layouts  5.84 us

profile of v3, /device:TPU:57, one launch (start us, length us, event | category | flops | bytes accessed | tf_op | source)
XLA Modules:
  0.0 133.2 jit_solution(2239541894096571890)
XLA Ops:
  0.6 0.0 copy-start
  0.6 1.9 %copy-done = f32[48,12,32,16]{0,3,2,1:T(8,128)S(1)} copy-done((f32[48,12,32,16]{0,3,2,1:T(8,128)S(1)}, f32[48,12,32,16]{0,3,2,1:T(8,128)}, u32[]{:S(2)}) %copy-start) | copy-done | bytes 1179672
  2.5 0.0 copy-start.1
  2.5 0.9 copy-done.1
  3.4 0.0 copy-start.2
  3.4 0.9 copy-done.2
  4.3 126.2 %window.1 = (f32[48,96]{1,0:T(8,128)S(1)}, f32[12,96]{1,0:T(8,128)S(1)}, f32[32,3,192]{2,1,0:T(4,128)S(1)}) custom-call(f32[12,512,48]{2,1,0:T(8,128)S(1)} %bitcast.9, f32[96,384]{1,0:T(8,128)S(1)} %bitcast.10, f32[96,384]{1,0:T(8,128)S(1)} %bitcast.11), custom_call_target="tpu_custom_call" | custom-call | tf_op jit(solution)/shard_map/window/pallas_call | solution.py:334
  130.6 0.3 reshape.16
  130.9 0.2 copy.8
  131.1 0.9 copy.9
  132.0 0.6 copy.12
  132.6 0.6 copy.13
  (1 shorter events, 0.0 us)
Async XLA Ops:
  0.6 1.9 %copy-start = (f32[48,12,32,16]{0,3,2,1:T(8,128)S(1)}, f32[48,12,32,16]{0,3,2,1:T(8,128)}, u32[]{:S(2)}) copy-start(f32[48,12,32,16]{0,3,2,1:T(8,128)} %param.3) | copy-start | bytes 3538948
  2.5 0.9 copy-start.1
  3.4 0.9 copy-start.2

commit v4 on v3

--- a/solution.py
+++ b/solution.py
@@ -6,13 +6,13 @@
 from jax.sharding import PartitionSpec as P
 
 ITERS = 4
-HIGH = lax.Precision.HIGHEST
 MESH = pl.DeviceIdType.MESH
 F32 = jnp.float32
 BF16 = jnp.bfloat16
 
 NXC, NYC, NZC = 4, 4, 8
 GX, GY = 8, 32
+CHUNKS = 3
 PLANE = NXC * NYC
 
 
@@ -46,7 +46,7 @@
         pltpu.VMEM((PLANE, 24, 128), F32),
         pltpu.VMEM((PLANE, 24, 128), F32),
         pltpu.VMEM((NZC, 24, 128), F32),
-        pltpu.SemaphoreType.DMA((2, 2)),
+        pltpu.SemaphoreType.DMA((1 + PLANE, 2)),
         pltpu.SemaphoreType.DMA((2, 2, PLANE)),
         pltpu.SemaphoreType.DMA((2, NZC)),
     ]
@@ -98,45 +98,60 @@
             send_sem=plane_sem.at[1, 0, d], recv_sem=plane_sem.at[1, 1, d],
             device_id=device(z, (plane + d) % PLANE, core), device_id_type=MESH)
 
+    def forward(k):
+        return core_copy(out.at[core, k], out.at[core, k], 1 + k)
+
     loop(1, PLANE, lambda d: gather(d).start())
-    loop(1, PLANE, lambda d: gather(d).wait())
-    copy = core_copy(out.at[core], out.at[core], 1)
-    copy.start()
-    copy.wait()
+    forward(plane).start()
+
+    def pass_on(d):
+        gather(d).wait_recv()
+        forward((plane + PLANE - d) % PLANE).start()
+
+    loop(1, PLANE, pass_on)
+    loop(1, PLANE, lambda d: gather(d).wait_send())
+    loop(0, PLANE, lambda k: forward(k).wait())
 
 
 PAIRS = [(0, 0), (0, 1), (0, 2), (1, 1), (1, 2), (2, 2)]
 
 
-def gram_blocks(rows, part):
+def split(a):
+    hi = a.astype(BF16)
+    rest = a - hi.astype(F32)
+    mid = rest.astype(BF16)
+    return hi, mid, (rest - mid.astype(F32)).astype(BF16)
+
+
+def dot(a, b, turned=False):
+    dims = (((1,), (1 if turned else 0,)), ((), ()))
+
+    def term(i, j):
+        return lax.dot_general(a[i], b[j], dims, preferred_element_type=F32)
+
+    small = term(0, 2) + term(2, 0) + term(1, 1)
+    return term(0, 0) + (term(0, 1) + term(1, 0) + small)
+
+
+def gram_terms(rows):
+    high, mid, low = split(rows)
+
+    def term(a, b):
+        return lax.dot_general(a, b, (((1,), (1,)), ((), ())), preferred_element_type=F32)
+
+    return term(high, high) + term(mid, mid), term(high, mid) + term(high, low)
+
+
+def store_blocks(full, part):
     for k, (a, b) in enumerate(PAIRS):
-        block = lax.dot_general(
-            rows[128 * a:128 * a + 128, :], rows[128 * b:128 * b + 128, :],
-            (((1,), (1,)), ((), ())), precision=HIGH, preferred_element_type=F32)
         flat = k * 128
         while flat < k * 128 + 128:
             inside = flat % 24
             size = min(24 - inside, k * 128 + 128 - flat)
             slab = flat // 24
-            part[slab // PLANE, slab % PLANE, inside:inside + size, :] = block[flat - k * 128:flat - k * 128 + size]
+            row = 128 * a + flat - k * 128
+            part[slab // PLANE, slab % PLANE, inside:inside + size, :] = full[row:row + size, 128 * b:128 * b + 128]
             flat += size
-
-
-def split(a):
-    hi = a.astype(BF16)
-    rest = a - hi.astype(F32)
-    mid = rest.astype(BF16)
-    return hi, mid, (rest - mid.astype(F32)).astype(BF16)
-
-
-def dot(a, b, turned=False):
-    dims = (((1,), (1 if turned else 0,)), ((), ()))
-
-    def term(i, j):
-        return lax.dot_general(a[i], b[j], dims, preferred_element_type=F32)
-
-    small = term(0, 2) + term(2, 0) + term(1, 1)
-    return term(0, 0) + (term(0, 1) + term(1, 0) + small)
 
 
 def inverse_factor(cross, panel=16):
@@ -223,51 +238,67 @@
     signal(barrier, device(z, plane, 1 - core))
     loop(1, PLANE, lambda d: signal(barrier, device(z, (plane + d) % PLANE, core)))
     loop(1, NZC, lambda d: signal(barrier, device((z + d) % NZC, plane, core)))
-    loop(1, GY, lambda d: signal(barrier, (gx, (gy + d) % GY)))
-    loop(0, GY, lambda k: signal(barrier, (k // 4, gx * 4 + k % 4)))
-    return GX - 1 + 1 + PLANE - 1 + NZC - 1 + GY - 1 + GY
-
-
-def window_kernel(cells, start_x, start_y, own_x, own_y, out, send_x, field, send_y, planes, rows, send_c,
-                  basis, gram, sem_x, sem_y, sem_c, *sums):
+    return GX - 1 + 1 + PLANE - 1 + NZC - 1
+
+
+def window_kernel(cells_hbm, start_x_hbm, start_y_hbm, own_x, own_y, out, cells, start_x, start_y, send_x, field,
+                  send_y, planes, rows, send_c, basis, gram, sem_in, sem_x, sem_y, sem_c, *sums):
     gx, gy, _, _, _ = position()
     sums_x, sums_y = sums[:len(sums) // 2], sums[len(sums) // 2:]
+
+    def fetch(h):
+        return pltpu.make_async_copy(cells_hbm.at[pl.ds(4 * h, 4)], cells.at[pl.ds(4 * h, 4)], sem_in.at[h])
+
+    starts = [
+        pltpu.make_async_copy(start_x_hbm, start_x, sem_in.at[CHUNKS]),
+        pltpu.make_async_copy(start_y_hbm, start_y, sem_in.at[CHUNKS + 1])]
+    for h in range(CHUNKS):
+        fetch(h).start()
+    for start in starts:
+        start.start()
     barrier = pltpu.get_barrier_semaphore()
     count = greet(barrier)
 
-    def turn(to):
-        for k in range(6):
-            start = pl.multiple_of(to * 64, 64)
-            pair = [cells[2 * k + h, pl.ds(start, 64), :] for h in range(2)]
-            yield slice(128 * k, 128 * k + 128), jnp.concatenate(pair, axis=0).T
-
-    def push_x(d):
+    def turn(h, to, target):
+        first = pl.multiple_of(to * 64, 64)
+        for k in range(2):
+            pair = [cells[4 * h + 2 * k + i, pl.ds(first, 64), :] for i in range(2)]
+            target[:, 128 * k:128 * k + 128] = jnp.concatenate(pair, axis=0).T
+
+    def copy_x(h, d):
         to = (gx + d) % GX
-        for lanes, block in turn(to):
-            send_x[to, :, lanes] = block
-
-    def copy_x(d):
-        to = (gx + d) % GX
-        return pltpu.make_async_remote_copy(
-            src_ref=send_x.at[to], dst_ref=field.at[gx],
-            send_sem=sem_x.at[0, d], recv_sem=sem_x.at[1, d],
+        return pltpu.make_async_remote_copy(
+            src_ref=send_x.at[h, to], dst_ref=field.at[h, gx],
+            send_sem=sem_x.at[0, h, d], recv_sem=sem_x.at[1, h, d],
             device_id=(to, gy), device_id_type=MESH)
 
-    loop(1, GX, push_x)
-    for lanes, block in turn(gx):
-        field[gx, :, lanes] = block
-    pl.semaphore_wait(barrier, count)
-    loop(1, GX, lambda d: copy_x(d).start())
-    loop(1, GX, lambda d: copy_x(d).wait())
-    gram_blocks(field[...].reshape(384, 768), sums_x[0])
+    for h in range(CHUNKS):
+        fetch(h).wait()
+        loop(1, GX, lambda d: turn(h, (gx + d) % GX, send_x.at[h, (gx + d) % GX]))
+        if h == 0:
+            pl.semaphore_wait(barrier, count)
+        loop(1, GX, lambda d: copy_x(h, d).start())
+    for h in range(CHUNKS):
+        turn(h, gx, field.at[h, gx])
+    straight, crossed = 0.0, 0.0
+    for h in range(CHUNKS):
+        loop(1, GX, lambda d: copy_x(h, d).wait_recv())
+        terms = gram_terms(field[h].reshape(384, 256))
+        straight, crossed = straight + terms[0], crossed + terms[1]
+    store_blocks(straight + (crossed + crossed.T), sums_x[0])
     all_sum(*sums_x)
+    for h in range(CHUNKS):
+        loop(1, GX, lambda d: copy_x(h, d).wait_send())
+    for start in starts:
+        start.wait()
     iterate(sums_x[1], start_x, gram, basis)
     parts = split(basis[...])
     own_x[...] = own_rows(parts, gx * 48, 48)
 
-    reduced = dot(parts, split(field[...].reshape(384, 768)))
-    for k in range(GY):
-        send_y[k] = reduced[3 * k:3 * k + 3, :]
+    for h in range(CHUNKS):
+        reduced = dot(parts, split(field[h].reshape(384, 256)))
+        for k in range(GY):
+            send_y[k, :, 256 * h:256 * h + 256] = reduced[3 * k:3 * k + 3, :]
 
     def copy_y(d):
         to = (gy + d) % GY
@@ -284,7 +315,8 @@
         pieces.append(jnp.zeros((GY, 64), F32))
         for k in range(2):
             rows[k, pl.ds(y, GY, stride=12), :] = jnp.concatenate(pieces[2 * k:2 * k + 2], axis=1)
-    gram_blocks(jnp.concatenate([rows[0], rows[1]], axis=1), sums_y[0])
+    straight, crossed = gram_terms(jnp.concatenate([rows[0], rows[1]], axis=1))
+    store_blocks(straight + (crossed + crossed.T), sums_y[0])
     all_sum(*sums_y)
     iterate(sums_y[1], start_y, gram, basis)
     parts = split(basis[...])
@@ -334,18 +366,22 @@
     own_x, own_y, pieces = pl.pallas_call(
         window_kernel,
         out_shape=[jax.ShapeDtypeStruct(shape, F32) for shape in ((48, 96), (12, 96), (GY, 3, 192))],
-        in_specs=[VM] * 3,
+        in_specs=[pl.BlockSpec(memory_space=pltpu.HBM)] * 3,
         out_specs=[VM] * 3,
         scratch_shapes=[
-            pltpu.VMEM((GX, 48, 768), F32),
-            pltpu.VMEM((GX, 48, 768), F32),
+            pltpu.VMEM((12, 512, 48), F32),
+            pltpu.VMEM((96, 384), F32),
+            pltpu.VMEM((96, 384), F32),
+            pltpu.VMEM((CHUNKS, GX, 48, 256), F32),
+            pltpu.VMEM((CHUNKS, GX, 48, 256), F32),
             pltpu.VMEM((GY, 3, 768), F32),
             pltpu.VMEM((GY, 3, 768), F32),
             pltpu.VMEM((2, 384, 128), F32),
             pltpu.VMEM((GY, 3, 192), F32),
             pltpu.VMEM((96, 384), F32),
             pltpu.VMEM((3, 384, 384), BF16),
-            pltpu.SemaphoreType.DMA((2, GX)),
+            pltpu.SemaphoreType.DMA((CHUNKS + 2,)),
+            pltpu.SemaphoreType.DMA((2, CHUNKS, GX)),
             pltpu.SemaphoreType.DMA((2, GY)),
             pltpu.SemaphoreType.DMA((2, GY)),
         ] + sum_scratch() + sum_scratch(),

time: 134 us -> 129 us (0.963)
  Pallas kernels: 126 us -> 122 us
    pallas_call x1, Pallas kernels: 126 us -> 122 us  [local(): pl.pallas_call(window_kernel, out_shape=[jax.ShapeDtypeStruct(shape, F32)...]
where the time goes in v4:
time: 129 us
  Pallas kernels  122 us (95%)
  local copies, waits for them, and re-layouts  6.33 us (5%)
    pallas_call x1, Pallas kernels, local(): pl.pallas_call(window_kernel, out_shape=[jax.ShapeDtypeStruct(shape, F32)...  122 us
    unnamed x9, local copies, waits for them, and re-layouts  5.84 us

profile of v4, /device:TPU:57, one launch (start us, length us, event | category | flops | bytes accessed | tf_op | source)
XLA Modules:
  0.0 128.6 jit_solution(4217496387796963719)
XLA Ops:
  0.6 0.0 copy-start
  0.6 1.9 %copy-done = f32[48,12,32,16]{0,3,2,1:T(8,128)S(1)} copy-done((f32[48,12,32,16]{0,3,2,1:T(8,128)S(1)}, f32[48,12,32,16]{0,3,2,1:T(8,128)}, u32[]{:S(2)}) %copy-start) | copy-done | bytes 1179672
  2.5 0.0 copy-start.1
  2.5 0.9 copy-done.1
  3.4 0.0 copy-start.2
  3.4 0.9 copy-done.2
  4.3 121.6 %window.1 = (f32[48,96]{1,0:T(8,128)S(1)}, f32[12,96]{1,0:T(8,128)S(1)}, f32[32,3,192]{2,1,0:T(4,128)S(1)}) custom-call(f32[12,512,48]{2,1,0:T(8,128)S(1)} %bitcast.9, f32[96,384]{1,0:T(8,128)S(1)} %bitcast.10, f32[96,384]{1,0:T(8,128)S(1)} %bitcast.11), custom_call_target="tpu_custom_call" | custom-call | tf_op jit(solution)/shard_map/window/pallas_call | solution.py:366
  126.0 0.3 reshape.16
  126.3 0.2 copy.8
  126.5 0.9 copy.9
  127.4 0.6 copy.12
  128.0 0.6 copy.13
  (1 shorter events, 0.0 us)
Async XLA Ops:
  0.6 1.9 %copy-start = (f32[48,12,32,16]{0,3,2,1:T(8,128)S(1)}, f32[48,12,32,16]{0,3,2,1:T(8,128)}, u32[]{:S(2)}) copy-start(f32[48,12,32,16]{0,3,2,1:T(8,128)} %param.3) | copy-start | bytes 3538948
  2.5 0.9 copy-start.1
  3.4 0.9 copy-start.2

commit v5 on v4

--- a/solution.py
+++ b/solution.py
@@ -125,12 +125,24 @@
 
 def dot(a, b, turned=False):
     dims = (((1,), (1 if turned else 0,)), ((), ()))
-
-    def term(i, j):
-        return lax.dot_general(a[i], b[j], dims, preferred_element_type=F32)
-
-    small = term(0, 2) + term(2, 0) + term(1, 1)
-    return term(0, 0) + (term(0, 1) + term(1, 0) + small)
+    n = a[0].shape[0]
+
+    def term(count, j):
+        left = a[0] if count == 1 else jnp.concatenate(a[:count], axis=0)
+        out = lax.dot_general(left, b[j], dims, preferred_element_type=F32)
+        return [out[n * i:n * i + n] for i in range(count)]
+
+    hh, mh, lh = term(3, 0)
+    hm, mm = term(2, 1)
+    hl, = term(1, 2)
+    return hh + (hm + mh + (hl + lh + mm))
+
+
+def dot_wide(a, b):
+    def wide(x, y, z, w):
+        return jnp.dot(jnp.concatenate([x, y], axis=1), jnp.concatenate([z, w], axis=0), preferred_element_type=F32)
+
+    return wide(a[0], a[1], b[0], b[0]) + (wide(a[0], a[1], b[1], b[1]) + wide(a[2], a[0], b[0], b[2]))
 
 
 def gram_terms(rows):
@@ -157,14 +169,15 @@
 def inverse_factor(cross, panel=16):
     rank = cross.shape[0]
     rows = lax.broadcasted_iota(jnp.int32, (panel, 128), 0)
-    left = cross
-    right = (lax.broadcasted_iota(jnp.int32, (rank, 128), 0)
-             == lax.broadcasted_iota(jnp.int32, (rank, 128), 1)).astype(F32)
+    lanes = lax.broadcasted_iota(jnp.int32, (panel, 128), 1)
+    here, rest = cross[:panel], cross[panel:]
     outs = []
     for first in range(0, rank, panel):
-        solved_left, solved_right, lower = left[:panel], right[:panel], right[:panel]
-        columns = [
-            jnp.broadcast_to(left[:panel, first + j:first + j + 1], (panel, 128)) for j in range(panel)]
+        end = first + panel
+        columns = [jnp.broadcast_to(here[:, first + j:first + j + 1], (panel, 128)) for j in range(panel)]
+        inside = (lanes >= first) & (lanes < end)
+        solved = jnp.where(inside, (rows + first == lanes).astype(F32), here)
+        lower = solved
         inverse = jnp.zeros((panel, 128), F32)
         for k in range(panel):
             pivot = 1.0 / jnp.broadcast_to(columns[k][k:k + 1], (panel, 128))
@@ -174,22 +187,28 @@
             inverse = jnp.where(rows == k, pivot, inverse)
             for j in range(k + 1, panel):
                 columns[j] = columns[j] - others * columns[j][k:k + 1]
-            solved_left = solved_left - others * solved_left[k:k + 1]
-            solved_right = solved_right - others * solved_right[k:k + 1]
+            solved = solved - others * solved[k:k + 1]
             lower = lower - below * lower[k:k + 1]
-        outs.append(lower * jnp.sqrt(inverse))
-        if first + panel == rank:
+        outs.append(jnp.where(lanes < end, lower * jnp.sqrt(inverse), 0.0))
+        if end == rank:
             break
-        solved = jnp.concatenate([solved_left * inverse, solved_right * inverse], axis=1)
+        solved = solved * inverse
+        after = rest[:panel]
+        here = jnp.where(inside, 0.0, after)
+        for k in range(panel):
+            here = here - jnp.broadcast_to(after[:, first + k:first + k + 1], (panel, 128)) * solved[k:k + 1]
+        rest = rest[panel:]
+        if end + panel == rank:
+            continue
 
         def place(block):
-            parts = [block, jnp.zeros((128 - first - panel, 256), BF16)]
+            parts = [block, jnp.zeros((128 - end, 128), BF16)]
             if first:
-                parts = [jnp.zeros((first, 256), BF16)] + parts
+                parts = [jnp.zeros((first, 128), BF16)] + parts
             return jnp.concatenate(parts, axis=0)
 
         high, mid, low = (place(t) for t in split(solved))
-        a_high, a_mid, a_low = split(left[panel:])
+        a_high, a_mid, a_low = split(rest)
 
         def wide(a, b, c, d):
             return jnp.dot(
@@ -198,8 +217,8 @@
 
         update = wide(a_high, a_mid, high, high) + (
             wide(a_high, a_mid, mid, mid) + wide(a_high, a_low, low, high))
-        left = left[panel:] - update[:, :128]
-        right = right[panel:] - update[:, 128:]
+        column = lax.broadcasted_iota(jnp.int32, update.shape, 1)
+        rest = jnp.where((column >= first) & (column < end), 0.0, rest) - update
     return jnp.concatenate(outs, axis=0)
 
 
@@ -218,7 +237,7 @@
         image = jnp.concatenate([image, jnp.zeros((32, 384), F32)], axis=0)
         parts = split(image)
         cross = dot([t[:96] for t in parts], parts, turned=True)
-        own[...] = dot(split(inverse_factor(cross)), parts)
+        own[...] = dot_wide(split(inverse_factor(cross)), parts)
 
     loop(0, ITERS, step)
 
@@ -386,7 +405,7 @@
             pltpu.SemaphoreType.DMA((2, GY)),
         ] + sum_scratch() + sum_scratch(),
         compiler_params=pltpu.CompilerParams(
-            collective_id=1, has_side_effects=True, vmem_limit_bytes=48 * 1024 * 1024),
+            collective_id=1, has_side_effects=True, vmem_limit_bytes=62 * 1024 * 1024),
         name="window",
     )(cells, start_x.T, start_y.T)
     pieces = pieces.reshape(8, 4, 3, 3, 4, 16)

time: 129 us -> 120 us (0.930)
  Pallas kernels: 122 us -> 115 us
  local copies, waits for them, and re-layouts: 6.33 us -> 4.96 us
    pallas_call x1, Pallas kernels: 122 us -> 115 us  [local(): pl.pallas_call(window_kernel, out_shape=[jax.ShapeDtypeStruct(shape, F32)...]
    unnamed x9 -> x3, local copies, waits for them, and re-layouts: 5.84 us -> 3.57 us
where the time goes in v5:
time: 120 us
  Pallas kernels  115 us (96%)
  local copies, waits for them, and re-layouts  4.96 us (4%)
    pallas_call x1, Pallas kernels, local(): pl.pallas_call(window_kernel, out_shape=[jax.ShapeDtypeStruct(shape, F32)...  115 us
    unnamed x3, local copies, waits for them, and re-layouts  3.57 us

profile of v5, /device:TPU:57, one launch (start us, length us, event | category | flops | bytes accessed | tf_op | source)
XLA Modules:
  0.0 120.3 jit_solution(6204549466032260182)
XLA Ops:
  0.6 114.7 %window.1 = (f32[48,96]{1,0:T(8,128)}, f32[12,96]{1,0:T(8,128)}, f32[32,3,192]{2,1,0:T(4,128)}) custom-call(f32[12,512,48]{2,1,0:T(8,128)} %bitcast.9, f32[96,384]{1,0:T(8,128)} %bitcast.12, f32[96,384]{1,0:T(8,128)} %bitcast.13), custom_call_target="tpu_custom_call" | custom-call | tf_op jit(solution)/shard_map/window/pallas_call | solution.py:385
  115.3 0.9 copy.7
  116.2 0.3 reshape.16
  116.6 0.2 copy.8
  116.7 0.9 copy.9
  117.7 1.3 %copy.12 = f32[48,96]{1,0:T(8,128)} copy(f32[48,96]{1,0:T(8,128)} %get-tuple-element.15) | data formatting | bytes 36864
  119.0 1.3 %copy.13 = f32[12,96]{1,0:T(8,128)} copy(f32[12,96]{1,0:T(8,128)} %get-tuple-element.16) | data formatting | bytes 9216

commit v6 on v5

--- a/solution.py
+++ b/solution.py
@@ -46,7 +46,7 @@
         pltpu.VMEM((PLANE, 24, 128), F32),
         pltpu.VMEM((PLANE, 24, 128), F32),
         pltpu.VMEM((NZC, 24, 128), F32),
-        pltpu.SemaphoreType.DMA((1 + PLANE, 2)),
+        pltpu.SemaphoreType.DMA((4 + PLANE, 2)),
         pltpu.SemaphoreType.DMA((2, 2, PLANE)),
         pltpu.SemaphoreType.DMA((2, NZC)),
     ]
@@ -60,20 +60,28 @@
             src_ref=src, dst_ref=dst, send_sem=core_sem.at[k, 0], recv_sem=core_sem.at[k, 1],
             device_id=device(z, plane, 1 - core), device_id_type=MESH)
 
-    copy = core_copy(part.at[1 - core], half, 0)
-    copy.start()
-    copy.wait()
-    half[...] += part[core]
-
-    def scatter(d):
-        to = (plane + d) % PLANE
+    def lend(row):
+        here = pl.ds(4 * row, 4)
+        return core_copy(part.at[1 - core, here], half.at[here], row)
+
+    def scatter(to):
+        d = (to + PLANE - plane) % PLANE
         return pltpu.make_async_remote_copy(
             src_ref=half.at[to], dst_ref=slots.at[d],
             send_sem=plane_sem.at[0, 0, d], recv_sem=plane_sem.at[0, 1, d],
             device_id=device(z, to, core), device_id_type=MESH)
 
-    loop(1, PLANE, lambda d: scatter(d).start())
-    loop(1, PLANE, lambda d: scatter(d).wait())
+    order = [(plane // 4 + e) % 4 for e in (2, 1, 3, 0)]
+    for row in order:
+        lend(row).start()
+    for e, row in enumerate(order):
+        lend(row).wait_recv()
+        here = pl.ds(4 * row, 4)
+        half[here] += part[core, here]
+        for i in range(1 if e == 3 else 0, 4):
+            scatter(4 * row + (plane + i) % 4).start()
+    loop(1, PLANE, lambda d: scatter((plane + d) % PLANE).wait())
+    loop(0, 4, lambda row: lend(row).wait_send())
     total = half[plane]
     for d in range(1, PLANE):
         total += slots[d]
@@ -99,7 +107,7 @@
             device_id=device(z, (plane + d) % PLANE, core), device_id_type=MESH)
 
     def forward(k):
-        return core_copy(out.at[core, k], out.at[core, k], 1 + k)
+        return core_copy(out.at[core, k], out.at[core, k], 4 + k)
 
     loop(1, PLANE, lambda d: gather(d).start())
     forward(plane).start()
@@ -145,9 +153,7 @@
     return wide(a[0], a[1], b[0], b[0]) + (wide(a[0], a[1], b[1], b[1]) + wide(a[2], a[0], b[0], b[2]))
 
 
-def gram_terms(rows):
-    high, mid, low = split(rows)
-
+def gram_terms(high, mid, low):
     def term(a, b):
         return lax.dot_general(a, b, (((1,), (1,)), ((), ())), preferred_element_type=F32)
 
@@ -260,7 +266,7 @@
     return GX - 1 + 1 + PLANE - 1 + NZC - 1
 
 
-def window_kernel(cells_hbm, start_x_hbm, start_y_hbm, own_x, own_y, out, cells, start_x, start_y, send_x, field,
+def window_kernel(cells_hbm, start_x_hbm, start_y_hbm, own_x, own_y, out, cells, start_x, start_y, send_x, field, field_terms,
                   send_y, planes, rows, send_c, basis, gram, sem_in, sem_x, sem_y, sem_c, *sums):
     gx, gy, _, _, _ = position()
     sums_x, sums_y = sums[:len(sums) // 2], sums[len(sums) // 2:]
@@ -279,10 +285,11 @@
     count = greet(barrier)
 
     def turn(h, to, target):
-        first = pl.multiple_of(to * 64, 64)
         for k in range(2):
-            pair = [cells[4 * h + 2 * k + i, pl.ds(first, 64), :] for i in range(2)]
-            target[:, 128 * k:128 * k + 128] = jnp.concatenate(pair, axis=0).T
+            slabs = [
+                cells[4 * h + 2 * k + i, pl.ds(pl.multiple_of(16 * (8 * z + to), 16), 16), :]
+                for i in range(2) for z in range(4)]
+            target[:, 128 * k:128 * k + 128] = jnp.concatenate(slabs, axis=0).T
 
     def copy_x(h, d):
         to = (gx + d) % GX
@@ -302,8 +309,11 @@
     straight, crossed = 0.0, 0.0
     for h in range(CHUNKS):
         loop(1, GX, lambda d: copy_x(h, d).wait_recv())
-        terms = gram_terms(field[h].reshape(384, 256))
-        straight, crossed = straight + terms[0], crossed + terms[1]
+        terms = split(field[h].reshape(384, 256))
+        for k in range(3):
+            field_terms[h, k] = terms[k]
+        more = gram_terms(*terms)
+        straight, crossed = straight + more[0], crossed + more[1]
     store_blocks(straight + (crossed + crossed.T), sums_x[0])
     all_sum(*sums_x)
     for h in range(CHUNKS):
@@ -312,10 +322,9 @@
         start.wait()
     iterate(sums_x[1], start_x, gram, basis)
     parts = split(basis[...])
-    own_x[...] = own_rows(parts, gx * 48, 48)
-
-    for h in range(CHUNKS):
-        reduced = dot(parts, split(field[h].reshape(384, 256)))
+
+    for h in range(CHUNKS):
+        reduced = dot(parts, [field_terms[h, k] for k in range(3)])
         for k in range(GY):
             send_y[k, :, 256 * h:256 * h + 256] = reduced[3 * k:3 * k + 3, :]
 
@@ -328,18 +337,18 @@
 
     loop(1, GY, lambda d: copy_y(d).start())
     planes[gy] = send_y[gy]
+    own_x[...] = own_rows(parts, gx * 48, 48)
     loop(1, GY, lambda d: copy_y(d).wait())
     for y in range(12):
         pieces = [planes[:, r, 64 * y:64 * y + 64] for r in range(3)]
         pieces.append(jnp.zeros((GY, 64), F32))
         for k in range(2):
             rows[k, pl.ds(y, GY, stride=12), :] = jnp.concatenate(pieces[2 * k:2 * k + 2], axis=1)
-    straight, crossed = gram_terms(jnp.concatenate([rows[0], rows[1]], axis=1))
+    straight, crossed = gram_terms(*split(jnp.concatenate([rows[0], rows[1]], axis=1)))
     store_blocks(straight + (crossed + crossed.T), sums_y[0])
     all_sum(*sums_y)
     iterate(sums_y[1], start_y, gram, basis)
     parts = split(basis[...])
-    own_y[...] = own_rows(parts, gy * 12, 12)
 
     core = dot(parts, split(jnp.concatenate([rows[0], rows[1]], axis=1)))
     for k in range(GY):
@@ -374,7 +383,19 @@
             copy_c(k, k).wait_recv()
 
     loop(0, GY, go)
+    own_y[...] = own_rows(parts, gy * 12, 12)
     loop(0, GY, finish)
+
+
+def results_kernel(own_x, own_y, pieces, basis_x, basis_y, core):
+    basis_x[...] = own_x[...]
+    basis_y[...] = own_y[...]
+    for j in range(4):
+        for s in range(3):
+            block = jnp.concatenate([pieces[4 * i + j, s:s + 1, :] for i in range(8)], axis=0).T
+            for r in range(3):
+                quarters = [block[64 * r + 16 * z:64 * r + 16 * z + 16] for z in range(4)]
+                core[3 * j + r, s] = jnp.concatenate(quarters, axis=1)
 
 
 VM = pl.BlockSpec(memory_space=pltpu.VMEM)
@@ -393,6 +414,7 @@
             pltpu.VMEM((96, 384), F32),
             pltpu.VMEM((CHUNKS, GX, 48, 256), F32),
             pltpu.VMEM((CHUNKS, GX, 48, 256), F32),
+            pltpu.VMEM((CHUNKS, 3, 384, 256), BF16),
             pltpu.VMEM((GY, 3, 768), F32),
             pltpu.VMEM((GY, 3, 768), F32),
             pltpu.VMEM((2, 384, 128), F32),
@@ -408,9 +430,15 @@
             collective_id=1, has_side_effects=True, vmem_limit_bytes=62 * 1024 * 1024),
         name="window",
     )(cells, start_x.T, start_y.T)
-    pieces = pieces.reshape(8, 4, 3, 3, 4, 16)
-    core = jnp.transpose(pieces, (1, 3, 2, 0, 4, 5)).reshape(12, 3, 32, 16)
-    return (own_x, own_y, core)
+    basis_x, basis_y, core = pl.pallas_call(
+        results_kernel,
+        out_shape=[jax.ShapeDtypeStruct(shape, F32) for shape in ((48, 96), (12, 96), (12, 3, 16, 32))],
+        in_specs=[VM] * 3,
+        out_specs=[VM] * 3,
+        compiler_params=pltpu.CompilerParams(vmem_limit_bytes=62 * 1024 * 1024),
+        name="results",
+    )(own_x, own_y, pieces)
+    return (basis_x, basis_y, jnp.transpose(core, (0, 1, 3, 2)))
 
 
 def solution(mesh):

time: 120 us -> 116 us (0.967)
  local copies, waits for them, and re-layouts: 4.96 us -> 0 us
    unnamed x3 -> x0, local copies, waits for them, and re-layouts: 3.57 us -> none
    pallas_call x0 -> x1, Pallas kernels: none -> 2.3 us  [local(): pl.pallas_call(results_kernel, out_shape=[jax.ShapeDtypeStruct(shape, F32...]
    pallas_call x1, Pallas kernels: 115 us -> 113 us  [local(): pl.pallas_call(window_kernel, out_shape=[jax.ShapeDtypeStruct(shape, F32)...]
where the time goes in v6:
time: 116 us
  Pallas kernels  116 us (100%)
    pallas_call x1, Pallas kernels, local(): pl.pallas_call(window_kernel, out_shape=[jax.ShapeDtypeStruct(shape, F32)...  113 us

profile of v6, /device:TPU:57, one launch (start us, length us, event | category | flops | bytes accessed | tf_op | source)
XLA Modules:
  0.0 116.4 jit_solution(11455046352215714593)
XLA Ops:
  0.6 113.4 %window.1 = (f32[48,96]{1,0:T(8,128)}, f32[12,96]{1,0:T(8,128)}, f32[32,3,192]{2,1,0:T(4,128)}) custom-call(f32[12,512,48]{2,1,0:T(8,128)} %bitcast.6, f32[96,384]{1,0:T(8,128)} %bitcast.7, f32[96,384]{1,0:T(8,128)} %bitcast.8), custom_call_target="tpu_custom_call" | custom-call | tf_op jit(solution)/shard_map/window/pallas_call | solution.py:406
  114.1 2.3 %results.1 = (f32[48,96]{1,0:T(8,128)}, f32[12,96]{1,0:T(8,128)}, f32[12,3,16,32]{3,2,1,0:T(8,128)}) custom-call(f32[48,96]{1,0:T(8,128)} %get-tuple-element.9.own_x, f32[12,96]{1,0:T(8,128)} %get-tuple-element.10.own_y, f32[32,3,192]{2,1,0:T(4,128)} %get-tuple-element.11.pieces), custom_call_target="tpu_custom_call" | custom-call | tf_op jit(solution)/shard_map/results/pallas_call | solution.py:433

commit v7 on v6

--- a/solution.py
+++ b/solution.py
@@ -14,6 +14,12 @@
 GX, GY = 8, 32
 CHUNKS = 3
 PLANE = NXC * NYC
+X_STEPS = ((1, 0), (1, 1), (0, 3), (1, 3), (0, 1), (1, 2), (0, 2))
+Y_STEPS = (
+    21, 20, 22, 23, 18, 19, 28, 13, 29, 17, 16, 12, 10, 15, 11, 14,
+    27, 31, 26, 30, 24, 4, 9, 25, 5, 8, 2, 6, 7, 3, 1)
+Z_STEPS = (4, 3, 5, 2, 6, 1, 7)
+PLANE_STEPS = (10, 6, 14, 9, 11, 2, 8, 5, 7, 13, 15, 1, 3, 4, 12)
 
 
 def position():
@@ -93,31 +99,33 @@
             send_sem=z_sem.at[0, d], recv_sem=z_sem.at[1, d],
             device_id=device((z + d) % NZC, plane, core), device_id_type=MESH)
 
-    loop(1, NZC, lambda d: spread(d).start())
+    for d in Z_STEPS:
+        spread(d).start()
     loop(1, NZC, lambda d: spread(d).wait())
     total = zslots[0]
     for k in range(1, NZC):
         total += zslots[k]
     out[core, plane] = total
 
-    def gather(d):
+    def beyond(step):
+        return (plane // 4 + step // 4) % 4 * 4 + (plane + step) % 4
+
+    def gather(step):
         return pltpu.make_async_remote_copy(
             src_ref=out.at[core, plane], dst_ref=out.at[core, plane],
-            send_sem=plane_sem.at[1, 0, d], recv_sem=plane_sem.at[1, 1, d],
-            device_id=device(z, (plane + d) % PLANE, core), device_id_type=MESH)
+            send_sem=plane_sem.at[1, 0, step], recv_sem=plane_sem.at[1, 1, step],
+            device_id=device(z, beyond(step), core), device_id_type=MESH)
 
     def forward(k):
         return core_copy(out.at[core, k], out.at[core, k], 4 + k)
 
-    loop(1, PLANE, lambda d: gather(d).start())
+    for step in PLANE_STEPS:
+        gather(step).start()
     forward(plane).start()
-
-    def pass_on(d):
-        gather(d).wait_recv()
-        forward((plane + PLANE - d) % PLANE).start()
-
-    loop(1, PLANE, pass_on)
-    loop(1, PLANE, lambda d: gather(d).wait_send())
+    for step in PLANE_STEPS[::-1]:
+        gather(step).wait_recv()
+        forward(beyond((4 - step // 4) % 4 * 4 + (4 - step % 4) % 4)).start()
+    loop(1, PLANE, lambda step: gather(step).wait_send())
     loop(0, PLANE, lambda k: forward(k).wait())
 
 
@@ -292,7 +300,7 @@
             target[:, 128 * k:128 * k + 128] = jnp.concatenate(slabs, axis=0).T
 
     def copy_x(h, d):
-        to = (gx + d) % GX
+        to = (gx // 4 + X_STEPS[d][0]) % 2 * 4 + (gx + X_STEPS[d][1]) % 4
         return pltpu.make_async_remote_copy(
             src_ref=send_x.at[h, to], dst_ref=field.at[h, gx],
             send_sem=sem_x.at[0, h, d], recv_sem=sem_x.at[1, h, d],
@@ -303,12 +311,14 @@
         loop(1, GX, lambda d: turn(h, (gx + d) % GX, send_x.at[h, (gx + d) % GX]))
         if h == 0:
             pl.semaphore_wait(barrier, count)
-        loop(1, GX, lambda d: copy_x(h, d).start())
+        for d in range(GX - 1):
+            copy_x(h, d).start()
     for h in range(CHUNKS):
         turn(h, gx, field.at[h, gx])
     straight, crossed = 0.0, 0.0
     for h in range(CHUNKS):
-        loop(1, GX, lambda d: copy_x(h, d).wait_recv())
+        for d in range(GX - 1):
+            copy_x(h, d).wait_recv()
         terms = split(field[h].reshape(384, 256))
         for k in range(3):
             field_terms[h, k] = terms[k]
@@ -317,7 +327,8 @@
     store_blocks(straight + (crossed + crossed.T), sums_x[0])
     all_sum(*sums_x)
     for h in range(CHUNKS):
-        loop(1, GX, lambda d: copy_x(h, d).wait_send())
+        for d in range(GX - 1):
+            copy_x(h, d).wait_send()
     for start in starts:
         start.wait()
     iterate(sums_x[1], start_x, gram, basis)
@@ -329,16 +340,19 @@
             send_y[k, :, 256 * h:256 * h + 256] = reduced[3 * k:3 * k + 3, :]
 
     def copy_y(d):
-        to = (gy + d) % GY
+        step = Y_STEPS[d]
+        to = (gy // 8 + step // 8) % 4 * 8 + (gy // 2 + step // 2) % 4 * 2 + (gy + step) % 2
         return pltpu.make_async_remote_copy(
             src_ref=send_y.at[to], dst_ref=planes.at[gy],
             send_sem=sem_y.at[0, d], recv_sem=sem_y.at[1, d],
             device_id=(gx, to), device_id_type=MESH)
 
-    loop(1, GY, lambda d: copy_y(d).start())
+    for d in range(GY - 1):
+        copy_y(d).start()
     planes[gy] = send_y[gy]
     own_x[...] = own_rows(parts, gx * 48, 48)
-    loop(1, GY, lambda d: copy_y(d).wait())
+    for d in range(GY - 1):
+        copy_y(d).wait()
     for y in range(12):
         pieces = [planes[:, r, 64 * y:64 * y + 64] for r in range(3)]
         pieces.append(jnp.zeros((GY, 64), F32))

time: 116 us -> 114 us (0.983)
  Pallas kernels: 116 us -> 113 us
    pallas_call x1, Pallas kernels: 113 us -> 111 us  [local(): pl.pallas_call(window_kernel, out_shape=[jax.ShapeDtypeStruct(shape, F32)...]
where the time goes in v7:
time: 114 us
  Pallas kernels  113 us (99%)
    pallas_call x1, Pallas kernels, local(): pl.pallas_call(window_kernel, out_shape=[jax.ShapeDtypeStruct(shape, F32)...  111 us
    pallas_call x1, Pallas kernels, local(): pl.pallas_call(results_kernel, out_shape=[jax.ShapeDtypeStruct(shape, F32...  2.3 us

profile of v7, /device:TPU:57, one launch (start us, length us, event | category | flops | bytes accessed | tf_op | source)
XLA Modules:
  0.0 113.5 jit_solution(4656636101359168362)
XLA Ops:
  0.6 110.6 %window.1 = (f32[48,96]{1,0:T(8,128)}, f32[12,96]{1,0:T(8,128)}, f32[32,3,192]{2,1,0:T(4,128)}) custom-call(f32[12,512,48]{2,1,0:T(8,128)} %bitcast.6, f32[96,384]{1,0:T(8,128)} %bitcast.7, f32[96,384]{1,0:T(8,128)} %bitcast.8), custom_call_target="tpu_custom_call" | custom-call | tf_op jit(solution)/shard_map/window/pallas_call | solution.py:420
  111.2 2.3 %results.1 = (f32[48,96]{1,0:T(8,128)}, f32[12,96]{1,0:T(8,128)}, f32[12,3,16,32]{3,2,1,0:T(8,128)}) custom-call(f32[48,96]{1,0:T(8,128)} %get-tuple-element.9.own_x, f32[12,96]{1,0:T(8,128)} %get-tuple-element.10.own_y, f32[32,3,192]{2,1,0:T(4,128)} %get-tuple-element.11.pieces), custom_call_target="tpu_custom_call" | custom-call | tf_op jit(solution)/shard_map/results/pallas_call | solution.py:447

commit v8 on v7

--- a/solution.py
+++ b/solution.py
@@ -168,15 +168,17 @@
     return term(high, high) + term(mid, mid), term(high, mid) + term(high, low)
 
 
-def store_blocks(full, part):
+def store_gram(straight, crossed, part):
     for k, (a, b) in enumerate(PAIRS):
+        rows, columns = slice(128 * a, 128 * a + 128), slice(128 * b, 128 * b + 128)
+        block = straight[rows, columns] + (crossed[rows, columns] + crossed[columns, rows].T)
         flat = k * 128
         while flat < k * 128 + 128:
             inside = flat % 24
             size = min(24 - inside, k * 128 + 128 - flat)
             slab = flat // 24
-            row = 128 * a + flat - k * 128
-            part[slab // PLANE, slab % PLANE, inside:inside + size, :] = full[row:row + size, 128 * b:128 * b + 128]
+            row = flat - k * 128
+            part[slab // PLANE, slab % PLANE, inside:inside + size, :] = block[row:row + size]
             flat += size
 
 
@@ -247,13 +249,23 @@
     own[...] = start[...]
 
     def step(_):
-        image = dot(split(own[...]), [gram[k] for k in range(3)])
-        image = jnp.concatenate([image, jnp.zeros((32, 384), F32)], axis=0)
-        parts = split(image)
-        cross = dot([t[:96] for t in parts], parts, turned=True)
+        parts, cross = image_of(gram, own)
         own[...] = dot_wide(split(inverse_factor(cross)), parts)
 
-    loop(0, ITERS, step)
+    loop(0, ITERS - 1, step)
+
+
+def image_of(gram, own):
+    image = dot(split(own[...]), [gram[k] for k in range(3)])
+    parts = split(jnp.concatenate([image, jnp.zeros((32, 384), F32)], axis=0))
+    return parts, dot([t[:96] for t in parts], parts, turned=True)
+
+
+def last_step(gram, own, others):
+    parts, cross = image_of(gram, own)
+    moved = [split(dot(parts, other)) for other in others]
+    inverse = split(inverse_factor(cross))
+    return [dot_wide(inverse, m) for m in moved], lambda: split(dot_wide(inverse, parts))
 
 
 def own_rows(parts, first, count):
@@ -279,6 +291,9 @@
     gx, gy, _, _, _ = position()
     sums_x, sums_y = sums[:len(sums) // 2], sums[len(sums) // 2:]
 
+    barrier = pltpu.get_barrier_semaphore()
+    count = greet(barrier)
+
     def fetch(h):
         return pltpu.make_async_copy(cells_hbm.at[pl.ds(4 * h, 4)], cells.at[pl.ds(4 * h, 4)], sem_in.at[h])
 
@@ -289,8 +304,6 @@
         fetch(h).start()
     for start in starts:
         start.start()
-    barrier = pltpu.get_barrier_semaphore()
-    count = greet(barrier)
 
     def turn(h, to, target):
         for k in range(2):
@@ -324,7 +337,7 @@
             field_terms[h, k] = terms[k]
         more = gram_terms(*terms)
         straight, crossed = straight + more[0], crossed + more[1]
-    store_blocks(straight + (crossed + crossed.T), sums_x[0])
+    store_gram(straight, crossed, sums_x[0])
     all_sum(*sums_x)
     for h in range(CHUNKS):
         for d in range(GX - 1):
@@ -332,10 +345,10 @@
     for start in starts:
         start.wait()
     iterate(sums_x[1], start_x, gram, basis)
-    parts = split(basis[...])
-
-    for h in range(CHUNKS):
-        reduced = dot(parts, [field_terms[h, k] for k in range(3)])
+
+    reduced_all, terms_x = last_step(
+        gram, basis, [[field_terms[h, k] for k in range(3)] for h in range(CHUNKS)])
+    for h, reduced in enumerate(reduced_all):
         for k in range(GY):
             send_y[k, :, 256 * h:256 * h + 256] = reduced[3 * k:3 * k + 3, :]
 
@@ -350,7 +363,7 @@
     for d in range(GY - 1):
         copy_y(d).start()
     planes[gy] = send_y[gy]
-    own_x[...] = own_rows(parts, gx * 48, 48)
+    own_x[...] = own_rows(terms_x(), gx * 48, 48)
     for d in range(GY - 1):
         copy_y(d).wait()
     for y in range(12):
@@ -359,12 +372,11 @@
         for k in range(2):
             rows[k, pl.ds(y, GY, stride=12), :] = jnp.concatenate(pieces[2 * k:2 * k + 2], axis=1)
     straight, crossed = gram_terms(*split(jnp.concatenate([rows[0], rows[1]], axis=1)))
-    store_blocks(straight + (crossed + crossed.T), sums_y[0])
+    store_gram(straight, crossed, sums_y[0])
     all_sum(*sums_y)
     iterate(sums_y[1], start_y, gram, basis)
-    parts = split(basis[...])
-
-    core = dot(parts, split(jnp.concatenate([rows[0], rows[1]], axis=1)))
+
+    (core,), terms_y = last_step(gram, basis, [split(jnp.concatenate([rows[0], rows[1]], axis=1))])
     for k in range(GY):
         send_c[k] = core[3 * k:3 * k + 3, :192]
     home = gy // 4
@@ -397,7 +409,7 @@
             copy_c(k, k).wait_recv()
 
     loop(0, GY, go)
-    own_y[...] = own_rows(parts, gy * 12, 12)
+    own_y[...] = own_rows(terms_y(), gy * 12, 12)
     loop(0, GY, finish)
 
 

time: 114 us -> 114 us (level)
  no operation moved by 1% of the time
where the time goes in v8:
time: 114 us
  Pallas kernels  113 us (99%)
    pallas_call x1, Pallas kernels, local(): pl.pallas_call(window_kernel, out_shape=[jax.ShapeDtypeStruct(shape, F32)...  111 us
    pallas_call x1, Pallas kernels, local(): pl.pallas_call(results_kernel, out_shape=[jax.ShapeDtypeStruct(shape, F32...  2.3 us

profile of v8, /device:TPU:57, one launch (start us, length us, event | category | flops | bytes accessed | tf_op | source)
XLA Modules:
  0.0 113.5 jit_solution(10584260296709226488)
XLA Ops:
  0.6 110.6 %window.1 = (f32[48,96]{1,0:T(8,128)}, f32[12,96]{1,0:T(8,128)}, f32[32,3,192]{2,1,0:T(4,128)}) custom-call(f32[12,512,48]{2,1,0:T(8,128)} %bitcast.6, f32[96,384]{1,0:T(8,128)} %bitcast.7, f32[96,384]{1,0:T(8,128)} %bitcast.8), custom_call_target="tpu_custom_call" | custom-call | tf_op jit(solution)/shard_map/window/pallas_call | solution.py:432
  111.2 2.3 %results.1 = (f32[48,96]{1,0:T(8,128)}, f32[12,96]{1,0:T(8,128)}, f32[12,3,16,32]{3,2,1,0:T(8,128)}) custom-call(f32[48,96]{1,0:T(8,128)} %get-tuple-element.9.own_x, f32[12,96]{1,0:T(8,128)} %get-tuple-element.10.own_y, f32[32,3,192]{2,1,0:T(4,128)} %get-tuple-element.11.pieces), custom_call_target="tpu_custom_call" | custom-call | tf_op jit(solution)/shard_map/results/pallas_call | solution.py:459

commit v9 on v8

--- a/solution.py
+++ b/solution.py
@@ -195,8 +195,15 @@
         solved = jnp.where(inside, (rows + first == lanes).astype(F32), here)
         lower = solved
         inverse = jnp.zeros((panel, 128), F32)
+        value = jnp.broadcast_to(columns[0][:1], (8, 128))
         for k in range(panel):
-            pivot = 1.0 / jnp.broadcast_to(columns[k][k:k + 1], (panel, 128))
+            pivot = 1.0 / value
+            if k + 1 < panel:
+                one, two, three = (
+                    jnp.broadcast_to(t, (8, 128))
+                    for t in (columns[k + 1][k + 1:k + 2], columns[k][k + 1:k + 2], columns[k + 1][k:k + 1]))
+                value = one - (two * three) * pivot
+            pivot = jnp.concatenate([pivot] * (panel // 8), axis=0)
             ratio = columns[k] * pivot
             others = jnp.where(rows == k, 0.0, ratio)
             below = jnp.where(rows > k, ratio, 0.0)
@@ -408,7 +415,7 @@
         def _():
             copy_c(k, k).wait_recv()
 
-    loop(0, GY, go)
+    loop(0, GY, lambda d: go((slot + d) % GY))
     own_y[...] = own_rows(terms_y(), gy * 12, 12)
     loop(0, GY, finish)
 

time: 114 us -> 113 us (level)
  no operation moved by 1% of the time
where the time goes in v9:
time: 113 us
  Pallas kernels  112 us (99%)
    pallas_call x1, Pallas kernels, local(): pl.pallas_call(window_kernel, out_shape=[jax.ShapeDtypeStruct(shape, F32)...  110 us
    pallas_call x1, Pallas kernels, local(): pl.pallas_call(results_kernel, out_shape=[jax.ShapeDtypeStruct(shape, F32...  2.3 us

profile of v9, /device:TPU:57, one launch (start us, length us, event | category | flops | bytes accessed | tf_op | source)
XLA Modules:
  0.0 113.0 jit_solution(17497321043378008855)
XLA Ops:
  0.6 110.1 %window.1 = (f32[48,96]{1,0:T(8,128)}, f32[12,96]{1,0:T(8,128)}, f32[32,3,192]{2,1,0:T(4,128)}) custom-call(f32[12,512,48]{2,1,0:T(8,128)} %bitcast.6, f32[96,384]{1,0:T(8,128)} %bitcast.7, f32[96,384]{1,0:T(8,128)} %bitcast.8), custom_call_target="tpu_custom_call" | custom-call | tf_op jit(solution)/shard_map/window/pallas_call | solution.py:439
  110.7 2.3 %results.1 = (f32[48,96]{1,0:T(8,128)}, f32[12,96]{1,0:T(8,128)}, f32[12,3,16,32]{3,2,1,0:T(8,128)}) custom-call(f32[48,96]{1,0:T(8,128)} %get-tuple-element.9.own_x, f32[12,96]{1,0:T(8,128)} %get-tuple-element.10.own_y, f32[32,3,192]{2,1,0:T(4,128)} %get-tuple-element.11.pieces), custom_call_target="tpu_custom_call" | custom-call | tf_op jit(solution)/shard_map/results/pallas_call | solution.py:466
